TPU v7x, 256 devices: a whole 4x4x8 slice. The times are simulated.
256 devices in a mesh: depth: 8 (over x, core), row: 32 (over y, z).
Axes of the slice: x: 4, y: 4, z: 8, core: 2. Of those that a mesh axis runs over, the one named last changes fastest.
Arguments:
- density: float32 [256, 1024, 2048], P('depth', 'row'), may hold values from 0.1 to 30
- emission: float32 [3], replicated, may hold values from 0.5 to 2
- absorption: float32 [1], replicated, may hold values from 0.15 to 0.6
Outputs:
- frame: float32 [4, 1024, 2048], P(None, 'row', 'depth')
All inputs are finite; a program needn't handle non-finite values.
Results may differ from a plain program's by a relative error of at most 0.000035.
Values sent between devices are 32-bit elements; how exact they have to be, the bound alone decides.
A program may use at most 64 MiB of HBM per device.

v0:
```python
import jax
import jax.numpy as jnp
from jax import lax
from jax.sharding import PartitionSpec as P


def extended(block, sides, width):
    for axis, dim in sides:
        count = lax.axis_size(axis)
        forward = [(i, i + 1) for i in range(count - 1)]
        backward = [(target, source) for source, target in forward]
        low = lax.ppermute(
            lax.slice_in_dim(block, block.shape[dim] - width, None, axis=dim), axis, forward
        )
        high = lax.ppermute(lax.slice_in_dim(block, 0, width, axis=dim), axis, backward)
        block = jnp.concatenate([low, block, high], axis=dim)
    return block


def from_partner(value, axis, apart):
    mask = 2**apart
    pairs = [(source, source ^ mask) for source in range(lax.axis_size(axis))]
    return lax.ppermute(value, axis, pairs)


def over_images(front_part, back_part):
    color = front_part[:3] + front_part[3:4] * back_part[:3]
    through = front_part[3:4] * back_part[3:4]
    return jnp.concatenate([color, through], axis=0)


def per_device(density, emission, absorption):
    depth_devices = lax.axis_size("depth")
    depth_total = density.shape[0] * depth_devices
    padded = extended(density, (("depth", 0), ("row", 1)), 1)
    cur = padded[1:-1, 1:-1]
    grad_z = (padded[2:, 1:-1] - padded[:-2, 1:-1]) * 0.5
    grad_y = (padded[1:-1, 2:] - padded[1:-1, :-2]) * 0.5
    padded_x = jnp.pad(cur, ((0, 0), (0, 0), (1, 1)))
    grad_x = (padded_x[:, :, 2:] - padded_x[:, :, :-2]) * 0.5
    along = jnp.abs(0.64 * grad_z + 0.6 * grad_y + 0.48 * grad_x)
    shade = 0.25 + 0.75 * along / jnp.sqrt(
        grad_z * grad_z + grad_y * grad_y + grad_x * grad_x + 1.0
    )
    tau = absorption[0] * cur / depth_total
    alpha = 1.0 - jnp.exp(-tau)
    running = jnp.cumsum(tau, axis=0)
    inside = running - tau
    lit = jnp.sum(jnp.exp(-inside) * alpha * shade, axis=0)
    through = jnp.exp(-running[-1])
    partial_image = jnp.concatenate([emission[:, None, None] * lit[None], through[None]], axis=0)
    row_count = partial_image.shape[1]
    width = partial_image.shape[2]
    piece_width = width // depth_devices
    levels = depth_devices.bit_length() - 1
    my_index = lax.axis_index("depth")
    current = partial_image.reshape((4, row_count) + (2,) * levels + (piece_width,))
    for level in range(levels):
        position = 2 + (levels - 1 - level)
        my_bit = my_index >> level & 1
        lower = jnp.take(current, 0, axis=position)
        upper = jnp.take(current, 1, axis=position)
        keeper = jnp.where(my_bit == 1, upper, lower)
        outgoing = jnp.where(my_bit == 1, lower, upper)
        incoming = from_partner(outgoing, "depth", level)
        front_part = jnp.where(my_bit == 1, incoming, keeper)
        back_part = jnp.where(my_bit == 1, keeper, incoming)
        current = over_images(front_part, back_part)
    opacity = 1.0 - current[3:4]
    return jnp.concatenate([current[:3], opacity], axis=0)


def solution(mesh):
    placed = (P("depth", "row", None), P(), P())
    return jax.shard_map(
        per_device, mesh=mesh, in_specs=placed, out_specs=P(None, "row", "depth"), check_vma=False
    )
```

profile of v0, /device:TPU:24, one launch (start us, length us, event | category | flops | bytes accessed | tf_op | source)
XLA Modules:
  0.0 85.0 jit_solution(12971253709159911226)
XLA Ops:
  0.0 1.1 %fusion.22 = (f32[1,32,2048]{2,1,0:T(8,128)S(1)}, f32[1,32,2048]{2,1,0:T(8,128)S(1)}) fusion(f32[32,32,2048]{2,1,0:T(8,128)} %param.15), kind=kLoop, calls=%fused_computation.66 | loop fusion | bytes 1048576 | tf_op jit(solution)/shard_map/slice | solution.py:15
  1.1 1.8 %collective-permute-start.1 = (f32[1,32,2048]{2,1,0:T(8,128)S(1)}, f32[1,32,2048]{2,1,0:T(8,128)S(1)}, u32[]{:S(2)}, u32[]{:S(2)}) collective-permute-start(f32[1,32,2048]{2,1,0:T(8,128)S(1)} %get-tuple-element.80), channel_id=1, source_target_pairs={{0,32},{32,64},{64,96},{96,128},{128,160},{160,192},{192,224},{1,3... | collective-permute-start | bytes 786440 | tf_op jit(solution)/shard_map/ppermute | solution.py:12
  2.8 1.3 %collective-permute-start = (f32[1,32,2048]{2,1,0:T(8,128)S(1)}, f32[1,32,2048]{2,1,0:T(8,128)S(1)}, u32[]{:S(2)}, u32[]{:S(2)}) collective-permute-start(f32[1,32,2048]{2,1,0:T(8,128)S(1)} %get-tuple-element.79), channel_id=1, source_target_pairs={{32,0},{64,32},{96,64},{128,96},{160,128},{192,160},{224,192},{33,... | collective-permute-start | bytes 786440 | tf_op jit(solution)/shard_map/ppermute | solution.py:15
  4.1 0.0 collective-permute-done.1
  4.2 4.0 %constant_dynamic-update-slice_fusion.1 = f32[34,32,2048]{2,1,0:T(8,128)S(1)} fusion(f32[34,32,2048]{2,1,0:T(8,128)S(1)} %constant_dynamic-update-slice_fusion.2, f32[32,32,2048]{2,1,0:T(8,128)} %param.15), kind=kLoop, calls=%fused_computation.62 | loop fusion | bytes 16777216
  8.1 0.0 collective-permute-done
  8.2 0.0 copy-start
  8.2 3.4 %copy-done = f32[34,32,2048]{2,1,0:T(8,128)} copy-done((f32[34,32,2048]{2,1,0:T(8,128)}, f32[34,32,2048]{2,1,0:T(8,128)S(1)}, u32[]{:S(2)}) %copy-start) | copy-done | bytes 8912920
  11.6 0.5 fusion.21
  12.1 7.9 %collective-permute-start.2 = (f32[34,1,2048]{2,1,0:T(1,128)S(1)}, f32[34,1,2048]{2,1,0:T(1,128)S(1)}, u32[]{:S(2)}, u32[]{:S(2)}) collective-permute-start(f32[34,1,2048]{2,1,0:T(1,128)S(1)} %get-tuple-element.77), channel_id=1, source_target_pairs={{1,0},{2,1},{3,2},{4,3},{5,4},{6,5},{7,6},{8,7},{9,8},{10,9},{11,1... | collective-permute-start | bytes 835592 | tf_op jit(solution)/shard_map/ppermute | solution.py:15
  20.1 1.9 %collective-permute-start.3 = (f32[34,1,2048]{2,1,0:T(1,128)S(1)}, f32[34,1,2048]{2,1,0:T(1,128)S(1)}, u32[]{:S(2)}, u32[]{:S(2)}) collective-permute-start(f32[34,1,2048]{2,1,0:T(1,128)S(1)} %get-tuple-element.78), channel_id=1, source_target_pairs={{0,1},{1,2},{2,3},{3,4},{4,5},{5,6},{6,7},{7,8},{8,9},{9,10},{10,1... | collective-permute-start | bytes 835592 | tf_op jit(solution)/shard_map/ppermute | solution.py:12
  22.6 1.5 %collective-permute-done.2 = f32[34,1,2048]{2,1,0:T(1,128)S(1)} collective-permute-done((f32[34,1,2048]{2,1,0:T(1,128)S(1)}, f32[34,1,2048]{2,1,0:T(1,128)S(1)}, u32[]{:S(2)}, u32[]{:S(2)}) %collective-permute-start.2) | collective-permute-done | bytes 278560 | tf_op jit(solution)/shard_map/ppermute | solution.py:15
  24.1 6.5 %collective-permute-done.3 = f32[34,1,2048]{2,1,0:T(1,128)S(1)} collective-permute-done((f32[34,1,2048]{2,1,0:T(1,128)S(1)}, f32[34,1,2048]{2,1,0:T(1,128)S(1)}, u32[]{:S(2)}, u32[]{:S(2)}) %collective-permute-start.3) | collective-permute-done | bytes 278560 | tf_op jit(solution)/shard_map/ppermute | solution.py:12
  30.7 28.7 %multiply_reduce_fusion = (f32[32,2048]{1,0:T(8,128)S(1)}, f32[32,32,2048]{2,1,0:T(8,128)}) fusion(f32[32,32,2048]{2,1,0:T(8,128)} %param.15, f32[34,32,2048]{2,1,0:T(8,128)} %copy-done, f32[34,1,2048]{2,1,0:T(1,128)S(1)} %collective-permute-done.3, f32[34,1,2048]{2,1,0:T(1,128)S(1)} %collective-permute-done.2, ...), kind=kOutput, calls=%fused_computation.9 | output fusion | flops 140443648 | bytes 35423232 | tf_op jit(solution)/shard_map/jit(cumsum)/reduce_window_sum | solution.py:47
  59.4 0.2 mul.128
  59.6 0.1 copy.5
  59.7 1.0 %fusion.13 = f32[1,32,2048]{2,1,0:T(8,128)S(1)} fusion(f32[32,32,2048]{2,1,0:T(8,128)} %get-tuple-element.94), kind=kLoop, calls=%fused_computation.30 | loop fusion | flops 65536 | bytes 524288 | tf_op jit(solution)/shard_map/exp | solution.py:50
  60.7 0.2 concatenate.36
  60.9 0.1 copy.6
  61.0 0.0 copy-done.1
  61.0 0.1 broadcast_multiply_fusion
  61.1 0.1 broadcast_select_fusion.3
  61.2 2.9 %collective-permute-start.4 = (f32[4,32,2,2,256]{4,1,0,2,3:T(8,128)S(1)}, f32[4,32,2,2,256]{4,1,0,2,3:T(8,128)S(1)}, u32[]{:S(2)}, u32[]{:S(2)}) collective-permute-start(f32[4,32,2,2,256]{4,1,0,2,3:T(8,128)S(1)} %broadcast_select_fusion.3), channel_id=1, source_target_pairs={{0,32},{32,0},{64,96},{96,64},{128,160},{160,128},{192,224},{224,1... | collective-permute-start | bytes 1572872 | tf_op jit(solution)/shard_map/ppermute | solution.py:23
  64.1 1.5 %collective-permute-done.4 = f32[4,32,2,2,256]{4,1,0,2,3:T(8,128)S(1)} collective-permute-done((f32[4,32,2,2,256]{4,1,0,2,3:T(8,128)S(1)}, f32[4,32,2,2,256]{4,1,0,2,3:T(8,128)S(1)}, u32[]{:S(2)}, u32[]{:S(2)}) %collective-permute-start.4) | collective-permute-done | bytes 524320 | tf_op jit(solution)/shard_map/ppermute | solution.py:23
  65.6 0.1 broadcast_select_fusion.1
  65.8 0.1 fusion.9
  65.9 5.0 %collective-permute-start.5 = (f32[4,32,2,256]{3,1,0,2:T(8,128)S(1)}, f32[4,32,2,256]{3,1,0,2:T(8,128)S(1)}, u32[]{:S(2)}, u32[]{:S(2)}) collective-permute-start(f32[4,32,2,256]{3,1,0,2:T(8,128)S(1)} %broadcast_select_fusion.7), channel_id=1, source_target_pairs={{0,64},{32,96},{64,0},{96,32},{128,192},{160,224},{192,128},{224,1... | collective-permute-start | bytes 786440 | tf_op jit(solution)/shard_map/ppermute | solution.py:23
  70.9 6.6 %collective-permute-done.5 = f32[4,32,2,256]{3,1,0,2:T(8,128)S(1)} collective-permute-done((f32[4,32,2,256]{3,1,0,2:T(8,128)S(1)}, f32[4,32,2,256]{3,1,0,2:T(8,128)S(1)}, u32[]{:S(2)}, u32[]{:S(2)}) %collective-permute-start.5) | collective-permute-done | bytes 262176 | tf_op jit(solution)/shard_map/ppermute | solution.py:23
  77.5 0.1 broadcast_select_fusion.5
  77.7 3.1 %collective-permute-start.6 = (f32[4,32,256]{2,1,0:T(8,128)S(1)}, f32[4,32,256]{2,1,0:T(8,128)S(1)}, u32[]{:S(2)}, u32[]{:S(2)}) collective-permute-start(f32[4,32,256]{2,1,0:T(8,128)S(1)} %broadcast_select_fusion.11), channel_id=1, source_target_pairs={{0,128},{32,160},{64,192},{96,224},{128,0},{160,32},{192,64},{224,... | collective-permute-start | bytes 393224 | tf_op jit(solution)/shard_map/ppermute | solution.py:23
  80.8 3.6 %collective-permute-done.6 = f32[4,32,256]{2,1,0:T(8,128)S(1)} collective-permute-done((f32[4,32,256]{2,1,0:T(8,128)S(1)}, f32[4,32,256]{2,1,0:T(8,128)S(1)}, u32[]{:S(2)}, u32[]{:S(2)}) %collective-permute-start.6) | collective-permute-done | bytes 131104 | tf_op jit(solution)/shard_map/ppermute | solution.py:23
  84.4 0.7 pad_maximum_fusion.7
  (11 shorter events, 0.2 us)
Async XLA Ops:
  1.1 3.1 %collective-permute-start.1 = (f32[1,32,2048]{2,1,0:T(8,128)S(1)}, f32[1,32,2048]{2,1,0:T(8,128)S(1)}, u32[]{:S(2)}, u32[]{:S(2)}) collective-permute-start(f32[1,32,2048]{2,1,0:T(8,128)S(1)} %get-tuple-element.80), channel_id=1, source_target_pairs={{0,32},{32,64},{64,96},{96,128},{128,160},{160,192},{192,224},{1,3... | collective-permute-start | bytes 786440 | tf_op jit(solution)/shard_map/ppermute | solution.py:12
  2.8 5.3 %collective-permute-start = (f32[1,32,2048]{2,1,0:T(8,128)S(1)}, f32[1,32,2048]{2,1,0:T(8,128)S(1)}, u32[]{:S(2)}, u32[]{:S(2)}) collective-permute-start(f32[1,32,2048]{2,1,0:T(8,128)S(1)} %get-tuple-element.79), channel_id=1, source_target_pairs={{32,0},{64,32},{96,64},{128,96},{160,128},{192,160},{224,192},{33,... | collective-permute-start | bytes 786440 | tf_op jit(solution)/shard_map/ppermute | solution.py:15
  8.2 3.4 %copy-start = (f32[34,32,2048]{2,1,0:T(8,128)}, f32[34,32,2048]{2,1,0:T(8,128)S(1)}, u32[]{:S(2)}) copy-start(f32[34,32,2048]{2,1,0:T(8,128)S(1)} %constant_dynamic-update-slice_fusion) | copy-start | bytes 26738692
  12.1 12.0 %collective-permute-start.2 = (f32[34,1,2048]{2,1,0:T(1,128)S(1)}, f32[34,1,2048]{2,1,0:T(1,128)S(1)}, u32[]{:S(2)}, u32[]{:S(2)}) collective-permute-start(f32[34,1,2048]{2,1,0:T(1,128)S(1)} %get-tuple-element.77), channel_id=1, source_target_pairs={{1,0},{2,1},{3,2},{4,3},{5,4},{6,5},{7,6},{8,7},{9,8},{10,9},{11,1... | collective-permute-start | bytes 835592 | tf_op jit(solution)/shard_map/ppermute | solution.py:15
  20.1 10.6 %collective-permute-start.3 = (f32[34,1,2048]{2,1,0:T(1,128)S(1)}, f32[34,1,2048]{2,1,0:T(1,128)S(1)}, u32[]{:S(2)}, u32[]{:S(2)}) collective-permute-start(f32[34,1,2048]{2,1,0:T(1,128)S(1)} %get-tuple-element.78), channel_id=1, source_target_pairs={{0,1},{1,2},{2,3},{3,4},{4,5},{5,6},{6,7},{7,8},{8,9},{9,10},{10,1... | collective-permute-start | bytes 835592 | tf_op jit(solution)/shard_map/ppermute | solution.py:12
  30.6 30.3 %copy-start.1 = (f32[3]{0:T(128)S(1)}, f32[3]{0:T(128)}, u32[]{:S(2)}) copy-start(f32[3]{0:T(128)} %param.16) | copy-start | bytes 40
  61.2 4.4 %collective-permute-start.4 = (f32[4,32,2,2,256]{4,1,0,2,3:T(8,128)S(1)}, f32[4,32,2,2,256]{4,1,0,2,3:T(8,128)S(1)}, u32[]{:S(2)}, u32[]{:S(2)}) collective-permute-start(f32[4,32,2,2,256]{4,1,0,2,3:T(8,128)S(1)} %broadcast_select_fusion.3), channel_id=1, source_target_pairs={{0,32},{32,0},{64,96},{96,64},{128,160},{160,128},{192,224},{224,1... | collective-permute-start | bytes 1572872 | tf_op jit(solution)/shard_map/ppermute | solution.py:23
  65.9 11.6 %collective-permute-start.5 = (f32[4,32,2,256]{3,1,0,2:T(8,128)S(1)}, f32[4,32,2,256]{3,1,0,2:T(8,128)S(1)}, u32[]{:S(2)}, u32[]{:S(2)}) collective-permute-start(f32[4,32,2,256]{3,1,0,2:T(8,128)S(1)} %broadcast_select_fusion.7), channel_id=1, source_target_pairs={{0,64},{32,96},{64,0},{96,32},{128,192},{160,224},{192,128},{224,1... | collective-permute-start | bytes 786440 | tf_op jit(solution)/shard_map/ppermute | solution.py:23
  77.7 6.6 %collective-permute-start.6 = (f32[4,32,256]{2,1,0:T(8,128)S(1)}, f32[4,32,256]{2,1,0:T(8,128)S(1)}, u32[]{:S(2)}, u32[]{:S(2)}) collective-permute-start(f32[4,32,256]{2,1,0:T(8,128)S(1)} %broadcast_select_fusion.11), channel_id=1, source_target_pairs={{0,128},{32,160},{64,192},{96,224},{128,0},{160,32},{192,64},{224,... | collective-permute-start | bytes 393224 | tf_op jit(solution)/shard_map/ppermute | solution.py:23
where the time goes:
time: 85.5 us; the launch traced here: 85 us
  other arithmetic  31 us (36%)
  starting transfers between devices  23.8 us (28%)
  waiting for transfers between devices  19.7 us (23%)
  local copies, waits for them, and re-layouts  9.6 us (11%)
  between operations  0.87 us (1%)
    another operation x1, other arithmetic, per_device(): running = jnp.cumsum(tau, axis=0)  28.7 us
    ppermute x3, waiting for transfers between devices, from_partner(): return lax.ppermute(value, axis, pairs)  11.7 us
    ppermute x3, starting transfers between devices, from_partner(): return lax.ppermute(value, axis, pairs)  10.9 us
    ppermute x2, starting transfers between devices, extended(): lax.ppermute(lax.slice_in_dim(block, 0, width, axis=dim), axis, backward)  9.24 us
    unnamed x6, local copies, waits for them, and re-layouts  7.41 us
    ppermute x2, waiting for transfers between devices, extended(): lax.ppermute(lax.slice_in_dim(block, block.shape[dim] - width, None, axis...  6.55 us
    ppermute x2, starting transfers between devices, extended(): lax.ppermute(lax.slice_in_dim(block, block.shape[dim] - width, None, axis...  3.68 us
  transfers between devices with their start and end apart: 7, of which 5 were waited for; matrix products, arithmetic and copies ran while one was open for 5% of the time, Pallas kernels for 0%

commit v1 on v0

v1 whole, which is shorter than its diff:
```python
import functools
import math

import jax
import jax.numpy as jnp
from jax import lax
from jax.experimental import pallas as pl
from jax.experimental.pallas import tpu as pltpu
from jax.sharding import PartitionSpec as P

MESH = pl.DeviceIdType.MESH
LANES = 128
TOP = 8


def chain(i, values):
    out = values[-1]
    for at in range(len(values) - 2, -1, -1):
        out = jnp.where(i == at, values[at], out)
    return out


def render(
    planes, rows, tiles, depth_total, absorption, density, out, vol, stage, recv,
    local_sem, zlo_send, zlo_recv, zhi_send, zhi_recv, ylo_send, ylo_recv, yhi_send, yhi_recv,
    piece_send, piece_recv,
):
    nd, nr = lax.axis_size("depth"), lax.axis_size("row")
    d, r = lax.axis_index("depth"), lax.axis_index("row")
    per_piece = tiles // nd
    body_z, body_y = pl.ds(1, planes), pl.ds(TOP, rows)

    def columns(xt):
        return pl.ds(pl.multiple_of(xt * LANES, LANES), LANES)

    def local_copy(xt):
        return pltpu.make_async_copy(
            density.at[:, :, columns(xt)], vol.at[xt + 1, body_z, body_y, :], local_sem.at[xt]
        )

    def z_copy(xt, up):
        source, target = (planes - 1, 0) if up else (0, planes + 1)
        send, got = (zlo_send, zlo_recv) if up else (zhi_send, zhi_recv)
        return pltpu.make_async_remote_copy(
            src_ref=density.at[source, :, columns(xt)], dst_ref=vol.at[xt + 1, target, body_y, :],
            send_sem=send.at[xt], recv_sem=got.at[xt],
            device_id={"depth": d + 1 if up else d - 1}, device_id_type=MESH,
        )

    def y_copy(xt, up):
        source, target = (rows - 1, TOP - 1) if up else (0, TOP + rows)
        send, got = (ylo_send, ylo_recv) if up else (yhi_send, yhi_recv)
        return pltpu.make_async_remote_copy(
            src_ref=density.at[:, pl.ds(source, 1), columns(xt)],
            dst_ref=vol.at[xt + 1, body_z, pl.ds(target, 1), :],
            send_sem=send.at[xt], recv_sem=got.at[xt],
            device_id={"row": r + 1 if up else r - 1}, device_id_type=MESH,
        )

    def piece_copy(target):
        return pltpu.make_async_remote_copy(
            src_ref=stage.at[target], dst_ref=recv.at[d],
            send_sem=piece_send.at[target], recv_sem=piece_recv.at[d],
            device_id={"depth": target}, device_id_type=MESH,
        )

    def piece_at(step):
        chip, core = d // 2, d % 2
        apart = chain(step, (2, 2, 1, 3, 1, 3, 0, 0))
        flip = chain(step, (0, 1, 0, 0, 1, 1, 1, 0))
        return (chip + apart) % (nd // 2) * 2 + (core + flip) % 2

    def each(count, body):
        def run(i, carry):
            body(i)
            return carry

        lax.fori_loop(0, count, run, 0)

    barrier = pltpu.get_barrier_semaphore()
    each(tiles, lambda xt: local_copy(xt).start())
    for step in range(1, nd):
        pl.semaphore_signal(barrier, inc=1, device_id={"depth": (d + step) % nd}, device_id_type=MESH)

    for step in (1, nr - 1):
        pl.semaphore_signal(barrier, inc=1, device_id={"row": (r + step) % nr}, device_id_type=MESH)

    vol[0, body_z, body_y, :] = jnp.zeros((planes, rows, LANES), jnp.float32)
    vol[tiles + 1, body_z, body_y, :] = jnp.zeros((planes, rows, LANES), jnp.float32)

    def clear_plane(z):
        def one(xt):
            vol[xt + 1, z, body_y, :] = jnp.zeros((rows, LANES), jnp.float32)

        each(tiles, one)

    def clear_row(y):
        def one(xt):
            vol[xt + 1, body_z, pl.ds(y, 1), :] = jnp.zeros((planes, 1, LANES), jnp.float32)

        each(tiles, one)

    pl.when(d == 0)(lambda: clear_plane(0))
    pl.when(d == nd - 1)(lambda: clear_plane(planes + 1))
    pl.when(r == 0)(lambda: clear_row(TOP - 1))
    pl.when(r == nr - 1)(lambda: clear_row(TOP + rows))

    pl.semaphore_wait(barrier, nd + 1)

    def start_halos(i):
        pl.when(d < nd - 1)(lambda: z_copy(i, True).start())
        pl.when(d > 0)(lambda: z_copy(i, False).start())
        xt = piece_at(i // per_piece) * per_piece + i % per_piece
        pl.when(r < nr - 1)(lambda: y_copy(xt, True).start())
        pl.when(r > 0)(lambda: y_copy(xt, False).start())

    each(tiles, start_halos)

    rate = absorption[0] * (-math.log2(math.e) / depth_total)
    lane = lax.broadcasted_iota(jnp.int32, (8, LANES), 1)
    is_first, is_last = lane == 0, lane == LANES - 1

    def cells(xt, starts):
        count = len(starts)

        def load(tile, z, start):
            return vol[tile, z, pl.ds(start, 8), :]

        def step(z, carry):
            before, cur, total, through, shine = ([*part] for part in carry)
            after = [load(xt + 1, z + 2, s) for s in starts]
            for i, s in enumerate(starts):
                c = cur[i]
                left = pltpu.roll(jnp.where(is_last, load(xt, z + 1, s), c), 1, 1)
                right = pltpu.roll(jnp.where(is_first, load(xt + 2, z + 1, s), c), LANES - 1, 1)
                dx = right - left
                dy = load(xt + 1, z + 1, s + 1) - load(xt + 1, z + 1, s - 1)
                dz = after[i] - before[i]
                along = jnp.abs(dz + 0.9375 * dy + 0.75 * dx)
                shade = along * lax.rsqrt(dz * dz + dy * dy + dx * dx + 4.0)
                total[i] = total[i] + c
                beyond = jnp.exp2(total[i] * rate)
                shine[i] = shine[i] + (through[i] - beyond) * shade
                through[i] = beyond
            return tuple(tuple(part) for part in (cur, after, total, through, shine))

        zero, one = jnp.zeros((8, LANES), jnp.float32), jnp.ones((8, LANES), jnp.float32)
        carry = (
            tuple(load(xt + 1, 0, s) for s in starts), tuple(load(xt + 1, 1, s) for s in starts),
            (zero,) * count, (one,) * count, (zero,) * count,
        )
        _, _, _, through, shine = lax.fori_loop(0, planes, step, carry, unroll=True)
        for i, s in enumerate(starts):
            piece, part = xt // per_piece, xt % per_piece
            stage[piece, 0, part, pl.ds(s - TOP, 8), :] = 0.25 * (1.0 - through[i]) + 0.48 * shine[i]
            stage[piece, 1, part, pl.ds(s - TOP, 8), :] = through[i]

    def inner(xt):
        pl.when(xt == 0)(lambda: local_copy(0).wait())
        pl.when(xt < tiles - 1)(lambda: local_copy(xt + 1).wait())
        pl.when(d > 0)(lambda: z_copy(xt, True).wait_recv())
        pl.when(d < nd - 1)(lambda: z_copy(xt, False).wait_recv())
        cells(xt, [TOP + 8 * i for i in range(1, rows // 8 - 1)])

    each(tiles, inner)

    def edges(i):
        piece = piece_at(i // per_piece)
        xt = piece * per_piece + i % per_piece
        pl.when(r > 0)(lambda: y_copy(xt, True).wait_recv())
        pl.when(r < nr - 1)(lambda: y_copy(xt, False).wait_recv())
        cells(xt, [TOP, TOP + rows - 8])
        ready = i % per_piece == per_piece - 1
        pl.when(ready & (piece != d))(lambda: piece_copy(piece).start())

    each(tiles, edges)

    recv[d] = stage[d]

    def drain(xt):
        pl.when(d < nd - 1)(lambda: z_copy(xt, True).wait_send())
        pl.when(d > 0)(lambda: z_copy(xt, False).wait_send())
        pl.when(r < nr - 1)(lambda: y_copy(xt, True).wait_send())
        pl.when(r > 0)(lambda: y_copy(xt, False).wait_send())

    each(tiles, drain)

    def arrived(step):
        other = (d + step + 1) % nd
        piece_copy(other).wait_send()
        pltpu.make_async_remote_copy(
            src_ref=stage.at[other], dst_ref=recv.at[other],
            send_sem=piece_send.at[other], recv_sem=piece_recv.at[other],
            device_id={"depth": other}, device_id_type=MESH,
        ).wait_recv()

    each(nd - 1, arrived)

    for part in range(per_piece):
        for y in range(0, rows, 8):
            at = pl.ds(y, 8)
            lit, through = recv[0, 0, part, at, :], recv[0, 1, part, at, :]
            for s in range(1, nd):
                lit = lit + through * recv[s, 0, part, at, :]
                through = through * recv[s, 1, part, at, :]
            out[0, at, pl.ds(part * LANES, LANES)] = lit
            out[1, at, pl.ds(part * LANES, LANES)] = through


def per_device(density, emission, absorption):
    nd = lax.axis_size("depth")
    planes, rows, width = density.shape
    tiles = width // LANES
    per_piece = tiles // nd
    sems = pltpu.SemaphoreType.DMA
    image = pl.pallas_call(
        functools.partial(render, planes, rows, tiles, planes * nd),
        out_shape=jax.ShapeDtypeStruct((2, rows, width // nd), jnp.float32),
        in_specs=[pl.BlockSpec(memory_space=pltpu.SMEM), pl.BlockSpec(memory_space=pl.ANY)],
        out_specs=pl.BlockSpec(memory_space=pltpu.VMEM),
        scratch_shapes=[
            pltpu.VMEM((tiles + 2, planes + 2, rows + 2 * TOP, LANES), jnp.float32),
            pltpu.VMEM((nd, 2, per_piece, rows, LANES), jnp.float32),
            pltpu.VMEM((nd, 2, per_piece, rows, LANES), jnp.float32),
            *[sems((tiles,))] * 9,
            *[sems((nd,))] * 2,
        ],
        compiler_params=pltpu.CompilerParams(
            collective_id=0, has_side_effects=True, vmem_limit_bytes=32 * 2**20
        ),
    )(absorption, density)
    lit, through = image[0], image[1]
    channel = lax.broadcasted_iota(jnp.int32, (4, 1, 1), 0)
    gain = jnp.concatenate([emission, jnp.zeros((1,), jnp.float32)])[:, None, None]
    return jnp.where(channel == 3, 1.0 - through[None], gain * lit[None])


def solution(mesh):
    placed = (P("depth", "row", None), P(), P())
    return jax.shard_map(
        per_device, mesh=mesh, in_specs=placed, out_specs=P(None, "row", "depth"), check_vma=False
    )
```

time: 85.5 us -> 33.2 us (0.39)
  the two profiles are of different devices: /device:TPU:24 before, /device:TPU:1 now
where the time goes in v1:
time: 33.2 us; the launch traced here: 33.1 us
  Pallas kernels  27.6 us (83%)
  local copies, waits for them, and re-layouts  3.38 us (10%)
  other arithmetic  1.48 us (4%)
  between operations  0.67 us (2%)
    pallas_call x1, Pallas kernels, per_device(): pl.pallas_call(functools.partial(render, planes, rows, tiles, planes * nd...  27.6 us
    unnamed x2, local copies, waits for them, and re-layouts  3.38 us
    select_n x1, other arithmetic, per_device(): return jnp.where(channel == 3, 1.0 - through[None], gain * lit[None])  0.74 us
    concatenate x1, other arithmetic, per_device(): jnp.concatenate([emission, jnp.zeros((1,), jnp.float32)])[:, None, None]  0.73 us

profile of v1, /device:TPU:1, one launch (start us, length us, event | category | flops | bytes accessed | tf_op | source)
XLA Modules:
  0.0 33.1 jit_solution(15203506436505526896)
XLA Ops:
  0.7 0.7 %pad_maximum_fusion = f32[4]{0:T(128)S(1)} fusion(f32[1]{0:T(128)} %constant.2.clone.1, f32[3]{0:T(128)} %param.4), kind=kLoop, calls=%fused_computation.3 | loop fusion | flops 4 | bytes 32 | tf_op jit(solution)/shard_map/concatenate | solution.py:234
  1.4 0.0 copy-start
  1.4 3.4 %copy-done = f32[32,32,2048]{2,1,0:T(8,128)S(1)} copy-done((f32[32,32,2048]{2,1,0:T(8,128)S(1)}, f32[32,32,2048]{2,1,0:T(8,128)}, u32[]{:S(2)}) %copy-start) | copy-done | bytes 8388632
  4.8 27.6 %shard_map.37 = f32[2,32,256]{2,1,0:T(8,128)S(1)} custom-call(f32[1]{0:T(128)S(6)} %copy.4.absorption, f32[32,32,2048]{2,1,0:T(8,128)S(1)} %copy-done), custom_call_target="tpu_custom_call" | custom-call | tf_op jit(solution)/shard_map/pallas_call | solution.py:216
  32.4 0.7 %multiply_select_fusion = f32[4,32,256]{2,1,0:T(8,128)} fusion(f32[32,256]{1,0:T(8,128)S(1)} %get-tuple-element.6, f32[4]{0:T(128)S(1)} %pad_maximum_fusion, f32[32,256]{1,0:T(8,128)S(1)} %get-tuple-element.5, pred[4]{0:T(512)(128)(4,1)S(1)} %iota_compare_fusion), kind=kLoop, calls=%fused_computation | loop fusion | flops 65536 | bytes 196628 | tf_op jit(solution)/shard_map/jit(_where)/select_n | solution.py:235
  (2 shorter events, 0.0 us)
Async XLA Ops:
  1.4 3.4 %copy-start = (f32[32,32,2048]{2,1,0:T(8,128)S(1)}, f32[32,32,2048]{2,1,0:T(8,128)}, u32[]{:S(2)}) copy-start(f32[32,32,2048]{2,1,0:T(8,128)} %density.1) | copy-start | bytes 25165828

commit v2 on v0

v2 whole, which is shorter than its diff:
```python
import functools
import math

import jax
import jax.numpy as jnp
from jax import lax
from jax.experimental import pallas as pl
from jax.experimental.pallas import tpu as pltpu
from jax.sharding import PartitionSpec as P

MESH = pl.DeviceIdType.MESH
LANES = 128
TOP = 8
APART = (2, 1, 3, 0)


def chain(i, values):
    out = values[-1]
    for at in range(len(values) - 2, -1, -1):
        out = jnp.where(i == at, values[at], out)
    return out


def each(count, body):
    def run(i, carry):
        body(i)
        return carry

    lax.fori_loop(0, count, run, 0)


def render(
    depth_total, absorption, emission, density, out, vol, near, far, mid, stage, merged, sibling, chips_in,
    local_sem, near_send, near_recv, far_send, far_recv, low_send, low_recv, high_send, high_recv,
    sib_send, sib_recv, out_send, out_recv,
):
    planes, groups, tiles = density.shape[:3]
    rows = 8 * groups
    last = planes - 1
    nd, nr = lax.axis_size("depth"), lax.axis_size("row")
    d, r = lax.axis_index("depth"), lax.axis_index("row")
    chips = nd // 2
    chip, core = d // 2, d % 2
    twin = d + 1 - 2 * core
    per_piece = tiles // nd
    inner_groups, edge_groups = range(1, groups - 1), (0, groups - 1)

    def tiles_of(piece):
        return pl.ds(piece * per_piece, per_piece)

    def local_copy(piece, g):
        return pltpu.make_async_copy(
            density.at[:, g, tiles_of(piece)],
            vol.at[:, pl.ds(piece * per_piece + 1, per_piece), pl.ds(TOP + 8 * g, 8), :],
            local_sem.at[piece, g],
        )

    def z_copy(up):
        send, got = (near_send, near_recv) if up else (far_send, far_recv)
        return pltpu.make_async_remote_copy(
            src_ref=density.at[last if up else 0], dst_ref=near if up else far,
            send_sem=send, recv_sem=got,
            device_id={"depth": d + 1 if up else d - 1}, device_id_type=MESH,
        )

    def y_copy(piece, up):
        g, y, target = (groups - 1, 7, TOP - 1) if up else (0, 0, TOP + rows)
        send, got = (low_send, low_recv) if up else (high_send, high_recv)
        return pltpu.make_async_remote_copy(
            src_ref=density.at[:, g, tiles_of(piece), y, :],
            dst_ref=vol.at[:, pl.ds(piece * per_piece + 1, per_piece), target, :],
            send_sem=send.at[piece], recv_sem=got.at[piece],
            device_id={"row": r + 1 if up else r - 1}, device_id_type=MESH,
        )

    def sibling_copy(target_chip, half):
        return pltpu.make_async_remote_copy(
            src_ref=stage.at[target_chip * 2 + 1 - core, half], dst_ref=sibling.at[target_chip, half],
            send_sem=sib_send.at[target_chip, half], recv_sem=sib_recv.at[target_chip, half],
            device_id={"depth": twin}, device_id_type=MESH,
        )

    def chip_copy(other, half, arriving=False):
        return pltpu.make_async_remote_copy(
            src_ref=merged.at[other, half], dst_ref=chips_in.at[other if arriving else chip, half],
            send_sem=out_send.at[other, half], recv_sem=out_recv.at[other if arriving else chip, half],
            device_id={"depth": other * 2 + core}, device_id_type=MESH,
        )

    def chip_at(step):
        return (chip + chain(step, APART)) % chips

    barrier = pltpu.get_barrier_semaphore()
    for peer in (twin, (d + 2) % nd, (d + 4) % nd, (d + 6) % nd, (d + nd - 1 + 2 * core) % nd):
        pl.semaphore_signal(barrier, inc=1, device_id={"depth": peer}, device_id_type=MESH)
    for peer in ((r + 1) % nr, (r + nr - 1) % nr):
        pl.semaphore_signal(barrier, inc=1, device_id={"row": peer}, device_id_type=MESH)

    def start_local(piece):
        for g in range(groups):
            local_copy(piece, g).start()

    each(nd, start_local)

    blank = jnp.zeros((planes, rows, LANES), jnp.float32)
    vol[:, 0, pl.ds(TOP, rows), :] = blank
    vol[:, tiles + 1, pl.ds(TOP, rows), :] = blank

    def clear_plane(ref):
        ref[...] = jnp.zeros(ref.shape, jnp.float32)

    def clear_row(y):
        def one(z):
            vol[z, :, y, :] = jnp.zeros((tiles + 2, LANES), jnp.float32)

        each(planes, one)

    pl.when(d == 0)(lambda: clear_plane(near))
    pl.when(d == nd - 1)(lambda: clear_plane(far))
    pl.when(r == 0)(lambda: clear_row(TOP - 1))
    pl.when(r == nr - 1)(lambda: clear_row(TOP + rows))

    pl.semaphore_wait(barrier, 7)
    pl.when(d < nd - 1)(lambda: z_copy(True).start())
    pl.when(d > 0)(lambda: z_copy(False).start())

    def piece_at(step):
        return chip_at(step % chips) * 2 + jnp.where(step < chips, 1 - core, core)

    def start_rows(step):
        piece = piece_at(step)
        pl.when(r < nr - 1)(lambda: y_copy(piece, True).start())
        pl.when(r > 0)(lambda: y_copy(piece, False).start())

    each(nd, start_rows)

    rate = absorption[0] * (-math.log2(math.e) / depth_total)
    lane = lax.broadcasted_iota(jnp.int32, (8, LANES), 1)
    is_first, is_last = lane == 0, lane == LANES - 1
    zero, one = jnp.zeros((8, LANES), jnp.float32), jnp.ones((8, LANES), jnp.float32)

    def load(tile, z, g, shift=0):
        return vol[z, tile + 1, pl.ds(TOP + 8 * g + shift, 8), :]

    def shading(unit, z, before, c, after):
        tile, g = unit
        left = pltpu.roll(jnp.where(is_last, load(tile - 1, z, g), c), 1, 1)
        right = pltpu.roll(jnp.where(is_first, load(tile + 1, z, g), c), LANES - 1, 1)
        dx = right - left
        dy = load(tile, z, g, 1) - load(tile, z, g, -1)
        dz = after - before
        along = jnp.abs(dz + 0.9375 * dy + 0.75 * dx)
        return along * lax.rsqrt(dz * dz + dy * dy + dx * dx + 4.0)

    def advance(units, z, carry, after):
        before, cur, total, through, shine = ([*part] for part in carry)
        for i, unit in enumerate(units):
            shade = shading(unit, z, before[i], cur[i], after[i])
            total[i] = total[i] + cur[i]
            beyond = jnp.exp2(total[i] * rate)
            shine[i] = shine[i] + (through[i] - beyond) * shade
            through[i] = beyond
        return tuple(tuple(part) for part in (cur, after, total, through, shine))

    def middle(units, carry):
        def step(z, carry):
            return advance(units, z, carry, [load(t, z + 1, g) for t, g in units])

        return lax.fori_loop(1, last, step, carry, unroll=True)

    def lit_of(through, shine):
        return 0.25 * (1.0 - through) + 0.48 * shine

    for g in range(groups):
        local_copy(0, g).wait()

    def inner(piece):
        @pl.when(piece < nd - 1)
        def _():
            for g in range(groups):
                local_copy(piece + 1, g).wait()

        units = [(piece * per_piece + part, g) for part in range(per_piece) for g in inner_groups]
        first = tuple(load(t, 0, g) for t, g in units)
        carry = (
            first, tuple(load(t, 1, g) for t, g in units), first,
            tuple(jnp.exp2(f * rate) for f in first), (zero,) * len(units),
        )
        _, cur, total, through, shine = middle(units, carry)
        for i, (t, g) in enumerate(units):
            at = pl.ds(8 * (g - 1), 8)
            beyond = jnp.exp2((total[i] + cur[i]) * rate)
            mid[t, 0, at, :] = shine[i]
            mid[t, 1, at, :] = beyond
            mid[t, 2, at, :] = through[i] - beyond

    each(nd, inner)

    def ends(piece):
        for part in range(per_piece):
            for g in inner_groups:
                tile = piece * per_piece + part
                unit, at = (tile, g), pl.ds(8 * (g - 1), 8)
                first = load(tile, 0, g)
                shine = mid[tile, 0, at, :]
                shine += (1.0 - jnp.exp2(first * rate)) * shading(unit, 0, near[g, tile], first, load(tile, 1, g))
                shine += mid[tile, 2, at, :] * shading(
                    unit, last, load(tile, last - 1, g), load(tile, last, g), far[g, tile]
                )
                through = mid[tile, 1, at, :]
                stage[piece, 0, 0, part, at, :] = lit_of(through, shine)
                stage[piece, 0, 1, part, at, :] = through

    def outer(piece):
        units = [(piece * per_piece + part, g) for part in range(per_piece) for g in edge_groups]
        carry = (
            tuple(near[g, t] for t, g in units), tuple(load(t, 0, g) for t, g in units),
            (zero,) * len(units), (one,) * len(units), (zero,) * len(units),
        )
        carry = advance(units, 0, carry, [load(t, 1, g) for t, g in units])
        carry = middle(units, carry)
        _, _, _, through, shine = advance(units, last, carry, [far[g, t] for t, g in units])
        for i, (t, g) in enumerate(units):
            part, at = i // 2, pl.ds(8 * (i % 2), 8)
            stage[piece, 1, 0, part, at, :] = lit_of(through[i], shine[i])
            stage[piece, 1, 1, part, at, :] = through[i]

    def wait_rows(piece):
        pl.when(r > 0)(lambda: y_copy(piece, True).wait_recv())
        pl.when(r < nr - 1)(lambda: y_copy(piece, False).wait_recv())

    def merge(target_chip, half):
        sibling_copy(target_chip, half).wait_recv()
        mine, other = stage.at[target_chip * 2 + core, half], sibling.at[target_chip, half]
        lit, through = mine[0], mine[1]
        lit_other, through_other = other[0], other[1]
        front = core == 0
        lit_all = jnp.where(front, lit, lit_other) + jnp.where(front, through, through_other) * jnp.where(
            front, lit_other, lit
        )
        through_all = through * through_other

        @pl.when(target_chip == chip)
        def _():
            chips_in[chip, half, 0] = lit_all
            chips_in[chip, half, 1] = through_all

        @pl.when(target_chip != chip)
        def _():
            merged[target_chip, half, 0] = lit_all
            merged[target_chip, half, 1] = through_all
            chip_copy(target_chip, half).start()

    pl.when(d > 0)(lambda: z_copy(True).wait_recv())
    pl.when(d < nd - 1)(lambda: z_copy(False).wait_recv())

    def for_sibling(step):
        target = chip_at(step)
        piece = target * 2 + 1 - core
        wait_rows(piece)
        ends(piece_at(2 * step))
        ends(piece_at(2 * step + 1))
        outer(piece)
        sibling_copy(target, 1).start()

        @pl.when(step < chips // 2)
        def _():
            sibling_copy(chip_at(2 * step), 0).start()
            sibling_copy(chip_at(2 * step + 1), 0).start()

    each(chips, for_sibling)
    each(chips, lambda step: merge(chip_at(step), 0))

    def for_chips(step):
        target = chip_at(step)
        piece = target * 2 + core
        wait_rows(piece)
        outer(piece)
        merge(target, 1)

    each(chips, for_chips)

    pl.when(d < nd - 1)(lambda: z_copy(True).wait_send())
    pl.when(d > 0)(lambda: z_copy(False).wait_send())

    def drain(piece):
        pl.when(r < nr - 1)(lambda: y_copy(piece, True).wait_send())
        pl.when(r > 0)(lambda: y_copy(piece, False).wait_send())

    each(nd, drain)

    def drain_sibling(target):
        for half in range(2):
            sibling_copy(target, half).wait_send()

    each(chips, drain_sibling)

    def arrived(step):
        other = (chip + 1 + step) % chips
        for half in range(2):
            chip_copy(other, half).wait_send()
            chip_copy(other, half, arriving=True).wait_recv()

    each(chips - 1, arrived)

    for half, which in enumerate((inner_groups, edge_groups)):
        for part in range(per_piece):
            for i, g in enumerate(which):
                at = pl.ds(8 * i, 8)
                lit, through = chips_in[0, half, 0, part, at, :], chips_in[0, half, 1, part, at, :]
                for s in range(1, chips):
                    lit = lit + through * chips_in[s, half, 0, part, at, :]
                    through = through * chips_in[s, half, 1, part, at, :]
                place = pl.ds(8 * g, 8), pl.ds(part * LANES, LANES)
                for c in range(3):
                    out[(c, *place)] = emission[c] * lit
                out[(3, *place)] = 1.0 - through


def per_device(density, emission, absorption):
    nd = lax.axis_size("depth")
    chips = nd // 2
    planes, rows, width = density.shape
    tiles, groups = width // LANES, rows // 8
    per_piece = tiles // nd
    tiled = density.reshape(planes, groups, 8, tiles, LANES).transpose(0, 1, 3, 2, 4)
    sem, real = pltpu.SemaphoreType.DMA, jnp.float32
    half = (2, 2, per_piece, rows // 2, LANES)
    return pl.pallas_call(
        functools.partial(render, planes * nd),
        out_shape=jax.ShapeDtypeStruct((4, rows, width // nd), real),
        in_specs=[pl.BlockSpec(memory_space=pltpu.SMEM)] * 2 + [pl.BlockSpec(memory_space=pl.ANY)],
        out_specs=pl.BlockSpec(memory_space=pltpu.VMEM),
        scratch_shapes=[
            pltpu.VMEM((planes, tiles + 2, rows + 2 * TOP, LANES), real),
            pltpu.VMEM((groups, tiles, 8, LANES), real),
            pltpu.VMEM((groups, tiles, 8, LANES), real),
            pltpu.VMEM((tiles, 3, rows // 2, LANES), real),
            pltpu.VMEM((nd, *half), real),
            pltpu.VMEM((chips, *half), real),
            pltpu.VMEM((chips, *half), real),
            pltpu.VMEM((chips, *half), real),
            sem((nd, groups)),
            *[sem] * 4,
            *[sem((nd,))] * 4,
            *[sem((chips, 2))] * 4,
        ],
        compiler_params=pltpu.CompilerParams(
            collective_id=0, has_side_effects=True, vmem_limit_bytes=57 * 2**20
        ),
    )(absorption, emission, tiled)


def solution(mesh):
    placed = (P("depth", "row", None), P(), P())
    return jax.shard_map(
        per_device, mesh=mesh, in_specs=placed, out_specs=P(None, "row", "depth"), check_vma=False
    )
```

time: 85.5 us -> 27.5 us (0.32)
  the two profiles are of different devices: /device:TPU:24 before, /device:TPU:1 now
where the time goes in v2:
time: 27.5 us; the launch traced here: 27.4 us
  Pallas kernels  25.2 us (92%)
  local copies, waits for them, and re-layouts  1.57 us (6%)
  between operations  0.66 us (2%)
    pallas_call x1, Pallas kernels, per_device(): pl.pallas_call(functools.partial(render, planes * nd), out_shape=jax.Shap...  25.2 us
    unnamed x1, local copies, waits for them, and re-layouts  1.57 us

profile of v2, /device:TPU:1, one launch (start us, length us, event | category | flops | bytes accessed | tf_op | source)
XLA Modules:
  0.0 27.4 jit_solution(12687023938820397220)
XLA Ops:
  0.7 25.2 %shard_map.37 = f32[4,32,256]{2,1,0:T(8,128)} custom-call(f32[1]{0:T(128)S(6)} %copy.5.absorption, f32[3]{0:T(128)} %emission.1, f32[32,4,16,8,128]{4,3,2,1,0:T(8,128)} %bitcast.3), custom_call_target="tpu_custom_call" | custom-call | tf_op jit(solution)/shard_map/pallas_call | solution.py:329
  25.8 1.6 %copy.6 = f32[4,32,256]{2,1,0:T(8,128)} copy(f32[4,32,256]{2,1,0:T(8,128)} %shard_map.37) | data formatting | bytes 262144

commit v3 on v2

v3 whole, which is shorter than its diff:
```python
import functools
import math

import jax
import jax.numpy as jnp
from jax import lax
from jax.experimental import pallas as pl
from jax.experimental.pallas import tpu as pltpu
from jax.sharding import PartitionSpec as P

MESH = pl.DeviceIdType.MESH
LANES = 128
LINE = 8
TOP = 8
APART = (2, 1, 3, 2, 1, 3, 0, 0)


def chain(i, values):
    out = values[-1]
    for at in range(len(values) - 2, -1, -1):
        out = jnp.where(i == at, values[at], out)
    return out


def each(count, body):
    def run(i, carry):
        body(i)
        return carry

    lax.fori_loop(0, count, run, 0)


def render(
    depth_total, absorption, emission_in, density, out, emission, vol, near, far, mid, stage, merged, sibling,
    chips_in, emission_sem, local_sem, near_send, near_recv, far_send, far_recv, low_send, low_recv, high_send, high_recv,
    sib_send, sib_recv, out_send, out_recv,
):
    planes, groups, tiles = density.shape[:3]
    rows = 8 * groups
    body_rows = pl.ds(TOP, rows)
    last = planes - 1
    nd, nr = lax.axis_size("depth"), lax.axis_size("row")
    d, r = lax.axis_index("depth"), lax.axis_index("row")
    chips = nd // 2
    chip, core = d // 2, d % 2
    twin = d + 1 - 2 * core
    per_piece = tiles // nd
    inner_groups, edge_groups = range(1, groups - 1), (0, groups - 1)

    def tiles_of(piece):
        return pl.ds(piece * per_piece, per_piece)

    def local_copy(piece, g):
        return pltpu.make_async_copy(
            density.at[:, g, tiles_of(piece)],
            vol.at[:, pl.ds(piece * per_piece + 1, per_piece), pl.ds(TOP + 8 * g, 8), :],
            local_sem.at[piece],
        )

    def wait_local(piece):
        block = vol.at[:, pl.ds(piece * per_piece + 1, per_piece), body_rows, :]
        pltpu.make_async_copy(block, block, local_sem.at[piece]).wait()

    def z_copy(piece, up):
        send, got = (near_send, near_recv) if up else (far_send, far_recv)
        return pltpu.make_async_remote_copy(
            src_ref=density.at[last if up else 0, :, tiles_of(piece)],
            dst_ref=(near if up else far).at[:, tiles_of(piece)],
            send_sem=send, recv_sem=got.at[piece],
            device_id={"depth": d + 1 if up else d - 1}, device_id_type=MESH,
        )

    def y_copy(piece, up):
        g, y, target = (groups - 1, 7, TOP - 1) if up else (0, 0, TOP + rows)
        send, got = (low_send, low_recv) if up else (high_send, high_recv)
        return pltpu.make_async_remote_copy(
            src_ref=density.at[:, g, tiles_of(piece), y, :],
            dst_ref=vol.at[:, pl.ds(piece * per_piece + 1, per_piece), target, :],
            send_sem=send, recv_sem=got.at[piece],
            device_id={"row": r + 1 if up else r - 1}, device_id_type=MESH,
        )

    def sibling_copy(target_chip, half):
        return pltpu.make_async_remote_copy(
            src_ref=stage.at[target_chip * 2 + 1 - core, half], dst_ref=sibling.at[target_chip, half],
            send_sem=sib_send, recv_sem=sib_recv.at[target_chip, half],
            device_id={"depth": twin}, device_id_type=MESH,
        )

    def chip_copy(other, half, arriving=False):
        return pltpu.make_async_remote_copy(
            src_ref=merged.at[other, half], dst_ref=chips_in.at[other if arriving else chip, half],
            send_sem=out_send, recv_sem=out_recv.at[other if arriving else chip, half],
            device_id={"depth": other * 2 + core}, device_id_type=MESH,
        )

    def order(step, device=d):
        mine = ((step >= chips - 1) & (step < nd - 2)) | (step == nd - 1)
        core = device % 2
        return (device // 2 + chain(step, APART)) % chips, jnp.where(mine, core, 1 - core)

    def piece_at(step, device=d):
        owner_chip, owner_core = order(step, device)
        return owner_chip * 2 + owner_core

    barrier = pltpu.get_barrier_semaphore()
    for peer in (twin, (d + 2) % nd, (d + 4) % nd, (d + 6) % nd, (d + nd - 1 + 2 * core) % nd):
        pl.semaphore_signal(barrier, inc=1, device_id={"depth": peer}, device_id_type=MESH)
    below, above = jnp.where(r > 0, 1, 0), jnp.where(r < nr - 1, 1, 0)

    @pl.when(r > 0)
    def _():
        pl.semaphore_signal(barrier, inc=1, device_id={"row": r - 1}, device_id_type=MESH)

    @pl.when(r < nr - 1)
    def _():
        pl.semaphore_signal(barrier, inc=1, device_id={"row": r + 1}, device_id_type=MESH)

    def start_local(piece):
        for g in range(groups):
            local_copy(piece, g).start()

    each(nd, start_local)
    emission_copy = pltpu.make_async_copy(emission_in, emission, emission_sem)
    emission_copy.start()

    blank = jnp.zeros((planes, rows, LANES), jnp.float32)
    vol[:, 0, pl.ds(TOP, rows), :] = blank
    vol[:, tiles + 1, pl.ds(TOP, rows), :] = blank

    def clear_plane(ref):
        ref[...] = jnp.zeros(ref.shape, jnp.float32)

    def clear_row(y):
        def one(z):
            vol[z, :, y, :] = jnp.zeros((tiles + 2, LANES), jnp.float32)

        each(planes, one)

    pl.when(d == 0)(lambda: clear_plane(near))
    pl.when(d == nd - 1)(lambda: clear_plane(far))
    pl.when(r == 0)(lambda: clear_row(TOP - 1))
    pl.when(r == nr - 1)(lambda: clear_row(TOP + rows))

    def start_halos(step):
        piece = piece_at(step)
        pl.when(d < nd - 1)(lambda: z_copy(piece_at(step, d + 1), True).start())
        pl.when(d > 0)(lambda: z_copy(piece_at(step, d - 1), False).start())
        pl.when(r < nr - 1)(lambda: y_copy(piece, True).start())
        pl.when(r > 0)(lambda: y_copy(piece, False).start())

    def open_links():
        pl.semaphore_wait(barrier, 5 + below + above)
        each(nd, start_halos)

    rate = absorption[0] * (-math.log2(math.e) / depth_total)
    lane = lax.broadcasted_iota(jnp.int32, (8, LANES), 1)
    is_first, is_last = lane == 0, lane == LANES - 1
    zero, one = jnp.zeros((8, LANES), jnp.float32), jnp.ones((8, LANES), jnp.float32)

    def load(tile, z, g, shift=0):
        return vol[z, tile + 1, pl.ds(TOP + 8 * g + shift, 8), :]

    def shading(unit, z, before, c, after):
        tile, g = unit
        left = pltpu.roll(jnp.where(is_last, load(tile - 1, z, g), c), 1, 1)
        right = pltpu.roll(jnp.where(is_first, load(tile + 1, z, g), c), LANES - 1, 1)
        dx = right - left
        dy = load(tile, z, g, 1) - load(tile, z, g, -1)
        dz = after - before
        along = jnp.abs(dz + 0.9375 * dy + 0.75 * dx)
        return along * lax.rsqrt(dz * dz + dy * dy + dx * dx + 4.0)

    def advance(units, z, carry, after):
        before, cur, total, through, shine = ([*part] for part in carry)
        for i, unit in enumerate(units):
            shade = shading(unit, z, before[i], cur[i], after[i])
            total[i] = total[i] + cur[i]
            beyond = jnp.exp2(total[i] * rate)
            shine[i] = shine[i] + (through[i] - beyond) * shade
            through[i] = beyond
        return tuple(tuple(part) for part in (cur, after, total, through, shine))

    def middle(units, carry):
        def step(z, carry):
            return advance(units, z, carry, [load(t, z + 1, g) for t, g in units])

        return lax.fori_loop(1, last, step, carry, unroll=True)

    def half_of(g):
        inside = g in inner_groups
        return int(not inside), pl.ds(8 * (inner_groups if inside else edge_groups).index(g), 8)

    def lit_of(through, shine):
        return 0.25 * (1.0 - through) + 0.48 * shine

    wait_local(0)
    opening = jnp.where((r % LINE == 0) & (r > 0), nd - 2, 0)

    def inner(piece):
        pl.when(piece == opening)(open_links)
        pl.when(piece < nd - 1)(lambda: wait_local(piece + 1))
        units = [(piece * per_piece + part, g) for part in range(per_piece) for g in inner_groups]
        first = tuple(load(t, 0, g) for t, g in units)
        carry = (
            first, tuple(load(t, 1, g) for t, g in units), first,
            tuple(jnp.exp2(f * rate) for f in first), (zero,) * len(units),
        )
        _, cur, total, through, shine = middle(units, carry)
        for i, (t, g) in enumerate(units):
            at = pl.ds(8 * (g - 1), 8)
            beyond = jnp.exp2((total[i] + cur[i]) * rate)
            mid[t, 0, at, :] = shine[i]
            mid[t, 1, at, :] = beyond
            mid[t, 2, at, :] = through[i] - beyond

    each(nd, inner)

    def store(piece, part, g, lit, through):
        half, at = half_of(g)
        stage[piece, half, 0, part, at, :] = lit
        stage[piece, half, 1, part, at, :] = through

    def ends(piece):
        for part in range(per_piece):
            for g in inner_groups:
                tile = piece * per_piece + part
                unit, at = (tile, g), pl.ds(8 * (g - 1), 8)
                first = load(tile, 0, g)
                shine = mid[tile, 0, at, :]
                shine += (1.0 - jnp.exp2(first * rate)) * shading(unit, 0, near[g, tile], first, load(tile, 1, g))
                shine += mid[tile, 2, at, :] * shading(
                    unit, last, load(tile, last - 1, g), load(tile, last, g), far[g, tile]
                )
                through = mid[tile, 1, at, :]
                store(piece, part, g, lit_of(through, shine), through)

    def outer(piece):
        units = [(piece * per_piece + part, g) for part in range(per_piece) for g in edge_groups]
        carry = (
            tuple(near[g, t] for t, g in units), tuple(load(t, 0, g) for t, g in units),
            (zero,) * len(units), (one,) * len(units), (zero,) * len(units),
        )
        carry = advance(units, 0, carry, [load(t, 1, g) for t, g in units])
        carry = middle(units, carry)
        _, _, _, through, shine = advance(units, last, carry, [far[g, t] for t, g in units])
        for i, (t, g) in enumerate(units):
            store(piece, i // 2, g, lit_of(through[i], shine[i]), through[i])

    def merge(target_chip, half):
        sibling_copy(target_chip, half).wait_recv()
        mine, other = stage.at[target_chip * 2 + core, half], sibling.at[target_chip, half]
        lit, through = mine[0], mine[1]
        lit_other, through_other = other[0], other[1]
        front = core == 0
        lit_all = jnp.where(front, lit, lit_other) + jnp.where(front, through, through_other) * jnp.where(
            front, lit_other, lit
        )
        return lit_all, through * through_other

    def dispatch(step, half):
        target, owner = order(step)

        @pl.when(owner != core)
        def _():
            sibling_copy(target, half).start()

        @pl.when((owner == core) & (target != chip))
        def _():
            merged[target, half, 0], merged[target, half, 1] = merge(target, half)
            chip_copy(target, half).start()

    def wait_planes(piece):
        pl.when(d > 0)(lambda: z_copy(piece, True).wait_recv())
        pl.when(d < nd - 1)(lambda: z_copy(piece, False).wait_recv())

    def wait_rows(piece):
        pl.when(r > 0)(lambda: y_copy(piece, True).wait_recv())
        pl.when(r < nr - 1)(lambda: y_copy(piece, False).wait_recv())

    wait_planes(piece_at(0))
    ends(piece_at(0))
    dispatch(0, 0)

    def outer_step(step):
        piece, later = piece_at(step), piece_at(jnp.minimum(step + 1, nd - 1))
        pl.when(step < nd - 1)(lambda: wait_planes(later))
        wait_rows(piece)
        ends(later)
        outer(piece)
        dispatch(step, 1)
        pl.when(step < nd - 1)(lambda: dispatch(step + 1, 0))

    each(nd, outer_step)

    def sent(ref, sem):
        pltpu.make_async_remote_copy(
            src_ref=ref, dst_ref=ref, send_sem=sem, recv_sem=out_recv.at[0, 0],
            device_id={"depth": twin}, device_id_type=MESH,
        ).wait_send()

    pl.when(d < nd - 1)(lambda: sent(near, near_send))
    pl.when(d > 0)(lambda: sent(far, far_send))
    halo_row = vol.at[:, pl.ds(1, tiles), TOP, :]
    pl.when(r < nr - 1)(lambda: sent(halo_row, low_send))
    pl.when(r > 0)(lambda: sent(halo_row, high_send))
    sent(sibling, sib_send)
    emission_copy.wait()

    for half, which in enumerate((inner_groups, edge_groups)):
        chips_in[chip, half, 0], chips_in[chip, half, 1] = merge(chip, half)
        each(chips - 1, lambda step: chip_copy((chip + 1 + step) % chips, half, arriving=True).wait_recv())
        for part in range(per_piece):
            for i, g in enumerate(which):
                at = pl.ds(8 * i, 8)
                lit, through = chips_in[0, half, 0, part, at, :], chips_in[0, half, 1, part, at, :]
                for s in range(1, chips):
                    lit = lit + through * chips_in[s, half, 0, part, at, :]
                    through = through * chips_in[s, half, 1, part, at, :]
                place = pl.ds(8 * g, 8), pl.ds(part * LANES, LANES)
                for c in range(3):
                    out[(c, *place)] = emission[c] * lit
                out[(3, *place)] = 1.0 - through
    sent(merged.at[pl.ds(0, chips - 1)], out_send)


def per_device(density, emission, absorption):
    nd = lax.axis_size("depth")
    chips = nd // 2
    planes, rows, width = density.shape
    tiles, groups = width // LANES, rows // 8
    per_piece = tiles // nd
    tiled = density.reshape(planes, groups, 8, tiles, LANES).transpose(0, 1, 3, 2, 4)
    sem, real = pltpu.SemaphoreType.DMA, jnp.float32
    piece = (2, 2, per_piece, rows // 2, LANES)
    return pl.pallas_call(
        functools.partial(render, planes * nd),
        out_shape=jax.ShapeDtypeStruct((4, rows, width // nd), real),
        in_specs=[pl.BlockSpec(memory_space=pltpu.SMEM)] + [pl.BlockSpec(memory_space=pl.ANY)] * 2,
        out_specs=pl.BlockSpec(memory_space=pltpu.VMEM),
        scratch_shapes=[
            pltpu.SMEM((3,), real),
            pltpu.VMEM((planes, tiles + 2, rows + 2 * TOP, LANES), real),
            pltpu.VMEM((groups, tiles, 8, LANES), real),
            pltpu.VMEM((groups, tiles, 8, LANES), real),
            pltpu.VMEM((tiles, 3, rows // 2, LANES), real),
            pltpu.VMEM((nd, *piece), real),
            pltpu.VMEM((chips, *piece), real),
            pltpu.VMEM((chips, *piece), real),
            pltpu.VMEM((chips, *piece), real),
            sem,
            sem((nd,)),
            *[sem, sem((nd,))] * 4,
            *[sem, sem((chips, 2))] * 2,
        ],
        compiler_params=pltpu.CompilerParams(
            collective_id=0, has_side_effects=True, vmem_limit_bytes=52 * 2**20
        ),
    )(absorption, emission, tiled)


def solution(mesh):
    placed = (P("depth", "row", None), P(), P())
    return jax.shard_map(
        per_device, mesh=mesh, in_specs=placed, out_specs=P(None, "row", "depth"), check_vma=False
    )
```

time: 27.5 us -> 20.6 us (0.75)
  the two profiles are of different devices: /device:TPU:1 before, /device:TPU:24 now
where the time goes in v3:
time: 20.6 us; the launch traced here: 20.5 us
  Pallas kernels  18.6 us (90%)
  local copies, waits for them, and re-layouts  1.31 us (6%)
  between operations  0.67 us (3%)
    pallas_call x1, Pallas kernels, per_device(): pl.pallas_call(functools.partial(render, planes * nd), out_shape=jax.Shap...  18.6 us
    unnamed x3, local copies, waits for them, and re-layouts  1.31 us

profile of v3, /device:TPU:24, one launch (start us, length us, event | category | flops | bytes accessed | tf_op | source)
XLA Modules:
  0.0 20.5 jit_solution(2076845742965793915)
XLA Ops:
  0.7 0.0 copy-start
  0.7 0.6 %copy-done = f32[3]{0:T(128)S(1)} copy-done((f32[3]{0:T(128)S(1)}, f32[3]{0:T(128)}, u32[]{:S(2)}) %copy-start) | copy-done | bytes 36
  1.3 18.6 %shard_map.37 = f32[4,32,256]{2,1,0:T(8,128)S(1)} custom-call(f32[1]{0:T(128)S(6)} %copy.5.absorption, f32[3]{0:T(128)S(1)} %copy-done, f32[32,4,16,8,128]{4,3,2,1,0:T(8,128)} %bitcast.3), custom_call_target="tpu_custom_call" | custom-call | tf_op jit(solution)/shard_map/pallas_call | solution.py:336
  19.9 0.7 %copy.6 = f32[4,32,256]{2,1,0:T(8,128)} copy(f32[4,32,256]{2,1,0:T(8,128)S(1)} %shard_map.37) | data formatting | bytes 262144
Async XLA Ops:
  0.7 0.7 %copy-start = (f32[3]{0:T(128)S(1)}, f32[3]{0:T(128)}, u32[]{:S(2)}) copy-start(f32[3]{0:T(128)} %emission_in.1) | copy-start | bytes 40

commit v4 on v3

v4 whole, which is shorter than its diff:
```python
import functools
import math

import jax
import jax.numpy as jnp
from jax import lax
from jax.experimental import pallas as pl
from jax.experimental.pallas import tpu as pltpu
from jax.sharding import PartitionSpec as P

MESH = pl.DeviceIdType.MESH
LANES = 128
HIGH, LOW, INNER = range(3)
LINE = 8
TOP = 8
APART = (2, 1, 3, 2, 1, 3, 0, 0)


def chain(i, values):
    out = values[-1]
    for at in range(len(values) - 2, -1, -1):
        out = jnp.where(i == at, values[at], out)
    return out


def each(count, body):
    def run(i, carry):
        body(i)
        return carry

    lax.fori_loop(0, count, run, 0)


def render(
    depth_total, absorption, emission_in, density, out, emission, vol, planes_in, mid, stage, merged,
    sibling, chips_in, emission_sem, local_sem, up_send, down_send, planes_recv, low_send, low_recv,
    high_send, high_recv, late_sem, sib_send, sib_recv, sib_own_recv, out_send, out_recv,
):
    planes, groups, tiles = density.shape[:3]
    rows = 8 * groups
    body_rows = pl.ds(TOP, rows)
    last = planes - 1
    nd, nr = lax.axis_size("depth"), lax.axis_size("row")
    d, r = lax.axis_index("depth"), lax.axis_index("row")
    chips = nd // 2
    chip, core = d // 2, d % 2
    twin = d + 1 - 2 * core
    per_piece = tiles // nd
    inner_groups = range(1, groups - 1)
    first_of_line = (r % LINE == 0) & (r > 0)
    last_of_line = (r % LINE == LINE - 1) & (r < nr - 1)
    PARTS = pl.ds(groups - 1, 1), pl.ds(0, 1), pl.ds(1, groups - 2)

    def tiles_of(piece):
        return pl.ds(piece * per_piece, per_piece)

    def local_copy(piece, g):
        return pltpu.make_async_copy(
            density.at[:, g, tiles_of(piece)],
            vol.at[:, pl.ds(piece * per_piece + 1, per_piece), pl.ds(TOP + 8 * g, 8), :],
            local_sem.at[piece],
        )

    def wait_local(piece):
        block = vol.at[:, pl.ds(piece * per_piece + 1, per_piece), body_rows, :]
        pltpu.make_async_copy(block, block, local_sem.at[piece]).wait()

    near, far = planes_in.at[0], planes_in.at[1]

    def z_copy(piece, up):
        return pltpu.make_async_remote_copy(
            src_ref=density.at[last if up else 0, :, tiles_of(piece)],
            dst_ref=(near if up else far).at[:, tiles_of(piece)],
            send_sem=up_send if up else down_send, recv_sem=planes_recv.at[piece],
            device_id={"depth": d + 1 if up else d - 1}, device_id_type=MESH,
        )

    def wait_planes(piece):
        def arrived(ref):
            pltpu.make_async_copy(ref, ref, planes_recv.at[piece]).wait()

        pl.when(d == 0)(lambda: arrived(far.at[:, tiles_of(piece)]))
        pl.when(d == nd - 1)(lambda: arrived(near.at[:, tiles_of(piece)]))
        pl.when((d > 0) & (d < nd - 1))(lambda: arrived(planes_in.at[:, :, tiles_of(piece)]))

    def y_copy(piece, up):
        g, y, target = (groups - 1, 7, TOP - 1) if up else (0, 0, TOP + rows)
        send, got = (low_send, low_recv) if up else (high_send, high_recv)
        return pltpu.make_async_remote_copy(
            src_ref=density.at[:, g, tiles_of(piece), y, :],
            dst_ref=vol.at[:, pl.ds(piece * per_piece + 1, per_piece), target, :],
            send_sem=send, recv_sem=got.at[piece],
            device_id={"row": r + 1 if up else r - 1}, device_id_type=MESH,
        )

    def sibling_copy(target_chip, part):
        return pltpu.make_async_remote_copy(
            src_ref=stage.at[target_chip * 2 + 1 - core, PARTS[part]],
            dst_ref=sibling.at[target_chip, PARTS[part]], send_sem=sib_send,
            recv_sem=sib_recv.at[target_chip, part], device_id={"depth": twin}, device_id_type=MESH,
        )

    def sibling_own_copy(part):
        return pltpu.make_async_remote_copy(
            src_ref=stage.at[twin, PARTS[part]], dst_ref=sibling.at[chip, PARTS[part]],
            send_sem=sib_send, recv_sem=sib_own_recv, device_id={"depth": twin}, device_id_type=MESH,
        )

    def chip_copy(other, part):
        return pltpu.make_async_remote_copy(
            src_ref=merged.at[other, PARTS[part]], dst_ref=chips_in.at[chip, PARTS[part]],
            send_sem=out_send, recv_sem=out_recv, device_id={"depth": other * 2 + core}, device_id_type=MESH,
        )

    def arrived(ref, sem):
        pltpu.make_async_copy(ref, ref, sem).wait()

    def order(step, device=d):
        mine = ((step >= chips - 1) & (step < nd - 2)) | (step == nd - 1)
        core = device % 2
        return (device // 2 + chain(step, APART)) % chips, jnp.where(mine, core, 1 - core)

    def piece_at(step, device=d):
        owner_chip, owner_core = order(step, device)
        return owner_chip * 2 + owner_core

    barrier = pltpu.get_barrier_semaphore()
    for peer in (twin, (d + 2) % nd, (d + 4) % nd, (d + 6) % nd, (d + nd - 1 + 2 * core) % nd):
        pl.semaphore_signal(barrier, inc=1, device_id={"depth": peer}, device_id_type=MESH)
    below = jnp.where((r > 0) & jnp.logical_not(first_of_line), 1, 0)
    above = jnp.where(r < nr - 1, 1, 0)

    @pl.when(r > 0)
    def _():
        pl.semaphore_signal(barrier, inc=1, device_id={"row": r - 1}, device_id_type=MESH)

    @pl.when((r < nr - 1) & jnp.logical_not(last_of_line))
    def _():
        pl.semaphore_signal(barrier, inc=1, device_id={"row": r + 1}, device_id_type=MESH)

    def start_local(piece):
        for g in range(groups):
            local_copy(piece, g).start()

    each(nd, start_local)
    emission_copy = pltpu.make_async_copy(emission_in, emission, emission_sem)
    emission_copy.start()

    blank = jnp.zeros((planes, rows, LANES), jnp.float32)
    vol[:, 0, pl.ds(TOP, rows), :] = blank
    vol[:, tiles + 1, pl.ds(TOP, rows), :] = blank

    def clear_plane(ref):
        ref[...] = jnp.zeros(ref.shape, jnp.float32)

    def clear_row(y):
        def one(z):
            vol[z, :, y, :] = jnp.zeros((tiles + 2, LANES), jnp.float32)

        each(planes, one)

    pl.when(d == 0)(lambda: clear_plane(near))
    pl.when(d == nd - 1)(lambda: clear_plane(far))
    pl.when(r == 0)(lambda: clear_row(TOP - 1))
    pl.when(r == nr - 1)(lambda: clear_row(TOP + rows))

    def start_halos(step):
        piece = piece_at(step)
        pl.when(d < nd - 1)(lambda: z_copy(piece_at(step, d + 1), True).start())
        pl.when(d > 0)(lambda: z_copy(piece_at(step, d - 1), False).start())
        pl.when(r < nr - 1)(lambda: y_copy(piece, True).start())
        pl.when((r > 0) & jnp.logical_not(first_of_line))(lambda: y_copy(piece, False).start())

    def start_late(step):
        y_copy(piece_at(step), False).start()

    def open_late():
        pl.semaphore_wait(late_sem, 1)
        each(nd, start_late)

    pl.semaphore_wait(barrier, 5 + below + above)

    @pl.when(last_of_line)
    def _():
        pl.semaphore_signal(late_sem, inc=1, device_id={"row": r + 1}, device_id_type=MESH)

    each(nd, start_halos)

    rate = absorption[0] * (-math.log2(math.e) / depth_total)
    lane = lax.broadcasted_iota(jnp.int32, (8, LANES), 1)
    is_first, is_last = lane == 0, lane == LANES - 1
    zero, one = jnp.zeros((8, LANES), jnp.float32), jnp.ones((8, LANES), jnp.float32)

    def load(tile, z, g, shift=0):
        return vol[z, tile + 1, pl.ds(TOP + 8 * g + shift, 8), :]

    def shading(unit, z, before, c, after):
        tile, g = unit
        left = pltpu.roll(jnp.where(is_last, load(tile - 1, z, g), c), 1, 1)
        right = pltpu.roll(jnp.where(is_first, load(tile + 1, z, g), c), LANES - 1, 1)
        dx = right - left
        dy = load(tile, z, g, 1) - load(tile, z, g, -1)
        dz = after - before
        along = jnp.abs(dz + 0.9375 * dy + 0.75 * dx)
        return along * lax.rsqrt(dz * dz + dy * dy + dx * dx + 4.0)

    def advance(units, z, carry, after):
        before, cur, total, through, shine = ([*part] for part in carry)
        for i, unit in enumerate(units):
            shade = shading(unit, z, before[i], cur[i], after[i])
            total[i] = total[i] + cur[i]
            beyond = jnp.exp2(total[i] * rate)
            shine[i] = shine[i] + (through[i] - beyond) * shade
            through[i] = beyond
        return tuple(tuple(part) for part in (cur, after, total, through, shine))

    def middle(units, carry):
        def step(z, carry):
            return advance(units, z, carry, [load(t, z + 1, g) for t, g in units])

        return lax.fori_loop(1, last, step, carry, unroll=True)

    def lit_of(through, shine):
        return 0.25 * (1.0 - through) + 0.48 * shine

    wait_local(0)

    def inner(piece):
        pl.when(piece < nd - 1)(lambda: wait_local(piece + 1))
        units = [(piece * per_piece + part, g) for part in range(per_piece) for g in inner_groups]
        first = tuple(load(t, 0, g) for t, g in units)
        carry = (
            first, tuple(load(t, 1, g) for t, g in units), first,
            tuple(jnp.exp2(f * rate) for f in first), (zero,) * len(units),
        )
        _, cur, total, through, shine = middle(units, carry)
        for i, (t, g) in enumerate(units):
            at = pl.ds(8 * (g - 1), 8)
            beyond = jnp.exp2((total[i] + cur[i]) * rate)
            mid[t, 0, at, :] = shine[i]
            mid[t, 1, at, :] = beyond
            mid[t, 2, at, :] = through[i] - beyond

    each(nd, inner)

    def store(piece, side, g, lit, through):
        stage[piece, g, 0, side] = lit
        stage[piece, g, 1, side] = through

    def ends(piece):
        for part in range(per_piece):
            for g in inner_groups:
                tile = piece * per_piece + part
                unit, at = (tile, g), pl.ds(8 * (g - 1), 8)
                first = load(tile, 0, g)
                shine = mid[tile, 0, at, :]
                shine += (1.0 - jnp.exp2(first * rate)) * shading(unit, 0, planes_in[0, g, tile], first, load(tile, 1, g))
                shine += mid[tile, 2, at, :] * shading(
                    unit, last, load(tile, last - 1, g), load(tile, last, g), planes_in[1, g, tile]
                )
                through = mid[tile, 1, at, :]
                store(piece, part, g, lit_of(through, shine), through)

    def outer(piece, g):
        units = [(piece * per_piece + part, g) for part in range(per_piece)]
        carry = (
            tuple(planes_in[0, g, t] for t, g in units), tuple(load(t, 0, g) for t, g in units),
            (zero,) * len(units), (one,) * len(units), (zero,) * len(units),
        )
        carry = advance(units, 0, carry, [load(t, 1, g) for t, g in units])
        carry = middle(units, carry)
        _, _, _, through, shine = advance(units, last, carry, [planes_in[1, g, t] for t, g in units])
        for side in range(per_piece):
            store(piece, side, g, lit_of(through[side], shine[side]), through[side])

    def merge(target_chip, part):
        mine, other = stage.at[target_chip * 2 + core, PARTS[part]], sibling.at[target_chip, PARTS[part]]
        lit, through = mine[:, 0], mine[:, 1]
        lit_other, through_other = other[:, 0], other[:, 1]
        front = core == 0
        lit_all = jnp.where(front, lit, lit_other) + jnp.where(front, through, through_other) * jnp.where(
            front, lit_other, lit
        )
        return lit_all, through * through_other

    def dispatch(step, part):
        target, owner = order(step)

        @pl.when((owner != core) & (target != chip))
        def _():
            sibling_copy(target, part).start()

        @pl.when((owner != core) & (target == chip))
        def _():
            sibling_own_copy(part).start()

        @pl.when((owner == core) & (target != chip))
        def _():
            sibling_copy(target, part).wait_recv()
            merged[target, PARTS[part], 0], merged[target, PARTS[part], 1] = merge(target, part)
            chip_copy(target, part).start()

    wait_planes(piece_at(0))
    ends(piece_at(0))
    dispatch(0, INNER)

    def high_step(step):
        piece, later = piece_at(step), piece_at(jnp.minimum(step + 1, nd - 1))
        pl.when(r < nr - 1)(lambda: y_copy(piece, False).wait_recv())
        ends(later)
        outer(piece, groups - 1)
        dispatch(step, HIGH)
        pl.when(step < nd - 1)(lambda: dispatch(step + 1, INNER))

    def low_step(step):
        piece = piece_at(step)
        pl.when(r > 0)(lambda: y_copy(piece, True).wait_recv())
        outer(piece, 0)
        dispatch(step, LOW)

    def outer_step(i):
        pl.when(first_of_line & (i == 3))(open_late)
        apart = first_of_line | last_of_line
        step = jnp.where(apart, i % nd, i // 2)
        low = jnp.where(first_of_line, i // nd, jnp.where(last_of_line, 1 - i // nd, i % 2))
        leads = low == jnp.where(last_of_line, 1, 0)
        pl.when(leads & (step < nd - 1))(lambda: wait_planes(piece_at(step + 1)))
        pl.when(low == 0)(lambda: high_step(step))
        pl.when(low == 1)(lambda: low_step(step))

    each(2 * nd, outer_step)

    def sent(ref, sem):
        pltpu.make_async_remote_copy(
            src_ref=ref, dst_ref=ref, send_sem=sem, recv_sem=out_recv,
            device_id={"depth": twin}, device_id_type=MESH,
        ).wait_send()

    pl.when(d < nd - 1)(lambda: sent(near, up_send))
    pl.when(d > 0)(lambda: sent(far, down_send))
    halo_row = vol.at[:, pl.ds(1, tiles), TOP, :]
    pl.when(r < nr - 1)(lambda: sent(halo_row, low_send))
    pl.when(r > 0)(lambda: sent(halo_row, high_send))
    sent(sibling, sib_send)
    emission_copy.wait()
    arrived(sibling.at[chip], sib_own_recv)
    for part in (HIGH, LOW, INNER):
        chips_in[chip, PARTS[part], 0], chips_in[chip, PARTS[part], 1] = merge(chip, part)
    others = merged.at[pl.ds(0, chips - 1)]
    sent(others, out_send)
    arrived(others, out_recv)

    def wait_planes(piece):
        pl.when(d > 0)(lambda: z_copy(piece, True).wait_recv())
        pl.when(d < nd - 1)(lambda: z_copy(piece, False).wait_recv())

    for g in range(groups):
        for side in range(per_piece):
            lit, through = chips_in[0, g, 0, side], chips_in[0, g, 1, side]
            for s in range(1, chips):
                lit = lit + through * chips_in[s, g, 0, side]
                through = through * chips_in[s, g, 1, side]
            place = pl.ds(8 * g, 8), pl.ds(side * LANES, LANES)
            for c in range(3):
                out[(c, *place)] = emission[c] * lit
            out[(3, *place)] = 1.0 - through


def per_device(density, emission, absorption):
    nd = lax.axis_size("depth")
    chips = nd // 2
    planes, rows, width = density.shape
    tiles, groups = width // LANES, rows // 8
    per_piece = tiles // nd
    tiled = density.reshape(planes, groups, 8, tiles, LANES).transpose(0, 1, 3, 2, 4)
    sem, real = pltpu.SemaphoreType.DMA, jnp.float32
    piece = (groups, 2, per_piece, 8, LANES)
    return pl.pallas_call(
        functools.partial(render, planes * nd),
        out_shape=jax.ShapeDtypeStruct((4, rows, width // nd), real),
        in_specs=[pl.BlockSpec(memory_space=pltpu.SMEM)] + [pl.BlockSpec(memory_space=pl.ANY)] * 2,
        out_specs=pl.BlockSpec(memory_space=pltpu.VMEM),
        scratch_shapes=[
            pltpu.SMEM((3,), real),
            pltpu.VMEM((planes, tiles + 2, rows + 2 * TOP, LANES), real),
            pltpu.VMEM((2, groups, tiles, 8, LANES), real),
            pltpu.VMEM((tiles, 3, rows // 2, LANES), real),
            pltpu.VMEM((nd, *piece), real),
            pltpu.VMEM((chips, *piece), real),
            pltpu.VMEM((chips, *piece), real),
            pltpu.VMEM((chips, *piece), real),
            sem,
            sem((nd,)),
            *[sem] * 2,
            sem((nd,)),
            *[sem, sem((nd,))] * 2,
            pltpu.SemaphoreType.REGULAR,
            sem,
            sem((chips, 3)),
            *[sem] * 3,
        ],
        compiler_params=pltpu.CompilerParams(
            collective_id=0, has_side_effects=True, vmem_limit_bytes=52 * 2**20
        ),
    )(absorption, *(pltpu.with_memory_space_constraint(x, pltpu.HBM) for x in (emission, tiled)))


def solution(mesh):
    placed = (P("depth", "row", None), P(), P())
    return jax.shard_map(
        per_device, mesh=mesh, in_specs=placed, out_specs=P(None, "row", "depth"), check_vma=False
    )
```

time: 20.6 us -> 19.4 us (0.942)
  local copies, waits for them, and re-layouts: 1.31 us -> 0.66 us
  Pallas kernels: 18.6 us -> 18 us
    unnamed x3 -> x1, local copies, waits for them, and re-layouts: 1.31 us -> 0.66 us
    pallas_call x1, Pallas kernels: 18.6 us -> 18 us  [per_device(): pl.pallas_call(functools.partial(render, planes * nd), out_shape=jax.Shap...]
where the time goes in v4:
time: 19.4 us; the launch traced here: 19.3 us
  Pallas kernels  18 us (93%)
  local copies, waits for them, and re-layouts  0.66 us (3%)
  between operations  0.66 us (3%)
    pallas_call x1, Pallas kernels, per_device(): pl.pallas_call(functools.partial(render, planes * nd), out_shape=jax.Shap...  18 us
    unnamed x1, local copies, waits for them, and re-layouts  0.66 us

profile of v4, /device:TPU:24, one launch (start us, length us, event | category | flops | bytes accessed | tf_op | source)
XLA Modules:
  0.0 19.3 jit_solution(4155518000675247559)
XLA Ops:
  0.7 18.0 %shard_map.37 = f32[4,32,256]{2,1,0:T(8,128)S(1)} custom-call(f32[1]{0:T(128)S(6)} %copy.5.absorption, f32[3]{0:T(128)} %emission_in.1, f32[32,4,16,8,128]{4,3,2,1,0:T(8,128)} %bitcast.3), custom_call_target="tpu_custom_call" | custom-call | tf_op jit(solution)/shard_map/pallas_call | solution.py:378
  18.7 0.7 %copy.6 = f32[4,32,256]{2,1,0:T(8,128)} copy(f32[4,32,256]{2,1,0:T(8,128)S(1)} %shard_map.37) | data formatting | bytes 262144

commit v5 on v4

--- a/solution.py
+++ b/solution.py
@@ -34,7 +34,7 @@
 def render(
     depth_total, absorption, emission_in, density, out, emission, vol, planes_in, mid, stage, merged,
     sibling, chips_in, emission_sem, local_sem, up_send, down_send, planes_recv, low_send, low_recv,
-    high_send, high_recv, late_sem, sib_send, sib_recv, sib_own_recv, out_send, out_recv,
+    high_send, high_recv, late_sem, twin_sem, sib_send, sib_recv, sib_own_recv, out_send, out_recv,
 ):
     planes, groups, tiles = density.shape[:3]
     rows = 8 * groups
@@ -49,6 +49,8 @@
     inner_groups = range(1, groups - 1)
     first_of_line = (r % LINE == 0) & (r > 0)
     last_of_line = (r % LINE == LINE - 1) & (r < nr - 1)
+    before_last = (r % LINE == LINE - 2) & (r < nr - 2)
+    greets, hears = last_of_line & (core == 0), last_of_line & (core == 1)
     PARTS = pl.ds(groups - 1, 1), pl.ds(0, 1), pl.ds(1, groups - 2)
 
     def tiles_of(piece):
@@ -125,18 +127,20 @@
         return owner_chip * 2 + owner_core
 
     barrier = pltpu.get_barrier_semaphore()
-    for peer in (twin, (d + 2) % nd, (d + 4) % nd, (d + 6) % nd, (d + nd - 1 + 2 * core) % nd):
-        pl.semaphore_signal(barrier, inc=1, device_id={"depth": peer}, device_id_type=MESH)
+
+    def signal(depth, row):
+        pl.semaphore_signal(barrier, inc=1, device_id={"depth": depth, "row": row}, device_id_type=MESH)
+
+    signal(twin, r)
+    for apart in range(1, chips):
+        signal((chip + apart) % chips * 2 + jnp.where(last_of_line, 1, core), r)
+    pl.when(jnp.logical_not(last_of_line))(lambda: signal((d + nd - 1 + 2 * core) % nd, r))
+    pl.when(r > 0)(lambda: signal(jnp.where(first_of_line, chip * 2, d), r - 1))
+    pl.when((r < nr - 1) & jnp.logical_not(last_of_line))(
+        lambda: signal(jnp.where(before_last, chip * 2 + 1, d), r + 1)
+    )
     below = jnp.where((r > 0) & jnp.logical_not(first_of_line), 1, 0)
     above = jnp.where(r < nr - 1, 1, 0)
-
-    @pl.when(r > 0)
-    def _():
-        pl.semaphore_signal(barrier, inc=1, device_id={"row": r - 1}, device_id_type=MESH)
-
-    @pl.when((r < nr - 1) & jnp.logical_not(last_of_line))
-    def _():
-        pl.semaphore_signal(barrier, inc=1, device_id={"row": r + 1}, device_id_type=MESH)
 
     def start_local(piece):
         for g in range(groups):
@@ -168,7 +172,7 @@
         piece = piece_at(step)
         pl.when(d < nd - 1)(lambda: z_copy(piece_at(step, d + 1), True).start())
         pl.when(d > 0)(lambda: z_copy(piece_at(step, d - 1), False).start())
-        pl.when(r < nr - 1)(lambda: y_copy(piece, True).start())
+        pl.when((r < nr - 1) & jnp.logical_not(last_of_line))(lambda: y_copy(piece, True).start())
         pl.when((r > 0) & jnp.logical_not(first_of_line))(lambda: y_copy(piece, False).start())
 
     def start_late(step):
@@ -178,12 +182,27 @@
         pl.semaphore_wait(late_sem, 1)
         each(nd, start_late)
 
-    pl.semaphore_wait(barrier, 5 + below + above)
+    def tell_twin():
+        pl.semaphore_signal(twin_sem, inc=1, device_id={"depth": twin}, device_id_type=MESH)
+
+    @pl.when(jnp.logical_not(hears))
+    def _():
+        pl.semaphore_wait(barrier, jnp.where(greets, 3, 5 + below + above))
+
+    pl.when(greets)(tell_twin)
+    pl.when(hears)(lambda: pl.semaphore_wait(twin_sem, 1))
 
     @pl.when(last_of_line)
     def _():
         pl.semaphore_signal(late_sem, inc=1, device_id={"row": r + 1}, device_id_type=MESH)
-
+        each(nd, lambda step: y_copy(piece_at(step), True).start())
+
+    @pl.when(hears)
+    def _():
+        pl.semaphore_wait(barrier, 2 * chips + 1)
+        tell_twin()
+
+    pl.when(greets)(lambda: pl.semaphore_wait(twin_sem, 1))
     each(nd, start_halos)
 
     rate = absorption[0] * (-math.log2(math.e) / depth_total)
@@ -319,7 +338,7 @@
         dispatch(step, LOW)
 
     def outer_step(i):
-        pl.when(first_of_line & (i == 3))(open_late)
+        pl.when(first_of_line & (i == 2))(open_late)
         apart = first_of_line | last_of_line
         step = jnp.where(apart, i % nd, i // 2)
         low = jnp.where(first_of_line, i // nd, jnp.where(last_of_line, 1 - i // nd, i % 2))
@@ -349,10 +368,6 @@
     others = merged.at[pl.ds(0, chips - 1)]
     sent(others, out_send)
     arrived(others, out_recv)
-
-    def wait_planes(piece):
-        pl.when(d > 0)(lambda: z_copy(piece, True).wait_recv())
-        pl.when(d < nd - 1)(lambda: z_copy(piece, False).wait_recv())
 
     for g in range(groups):
         for side in range(per_piece):
@@ -394,7 +409,7 @@
             *[sem] * 2,
             sem((nd,)),
             *[sem, sem((nd,))] * 2,
-            pltpu.SemaphoreType.REGULAR,
+            *[pltpu.SemaphoreType.REGULAR] * 2,
             sem,
             sem((chips, 3)),
             *[sem] * 3,

time: 19.4 us -> 18.8 us (0.969)
  Pallas kernels: 18 us -> 17.4 us
    pallas_call x1, Pallas kernels: 18 us -> 17.4 us  [per_device(): pl.pallas_call(functools.partial(render, planes * nd), out_shape=jax.Shap...]
where the time goes in v5:
time: 18.8 us; the launch traced here: 18.7 us
  Pallas kernels  17.4 us (93%)
  local copies, waits for them, and re-layouts  0.66 us (4%)
  between operations  0.66 us (4%)
    pallas_call x1, Pallas kernels, per_device(): pl.pallas_call(functools.partial(render, planes * nd), out_shape=jax.Shap...  17.4 us
    unnamed x1, local copies, waits for them, and re-layouts  0.66 us

profile of v5, /device:TPU:24, one launch (start us, length us, event | category | flops | bytes accessed | tf_op | source)
XLA Modules:
  0.0 18.7 jit_solution(3723000452757124382)
XLA Ops:
  0.7 17.4 %shard_map.37 = f32[4,32,256]{2,1,0:T(8,128)S(1)} custom-call(f32[1]{0:T(128)S(6)} %copy.5.absorption, f32[3]{0:T(128)} %emission_in.1, f32[32,4,16,8,128]{4,3,2,1,0:T(8,128)} %bitcast.3), custom_call_target="tpu_custom_call" | custom-call | tf_op jit(solution)/shard_map/pallas_call | solution.py:393
  18.0 0.7 %copy.6 = f32[4,32,256]{2,1,0:T(8,128)} copy(f32[4,32,256]{2,1,0:T(8,128)S(1)} %shard_map.37) | data formatting | bytes 262144

commit v6 on v5

--- a/solution.py
+++ b/solution.py
@@ -21,6 +21,12 @@
     for at in range(len(values) - 2, -1, -1):
         out = jnp.where(i == at, values[at], out)
     return out
+
+
+def lagging(count, lag):
+    ahead = [(2 * k, 0, k) for k in range(count)]
+    behind = [(2 * (k + lag) - 1, 1, k) for k in range(count)]
+    return [turn for _, *turn in sorted(ahead + behind)]
 
 
 def each(count, body):
@@ -339,11 +345,13 @@
 
     def outer_step(i):
         pl.when(first_of_line & (i == 2))(open_late)
-        apart = first_of_line | last_of_line
-        step = jnp.where(apart, i % nd, i // 2)
-        low = jnp.where(first_of_line, i // nd, jnp.where(last_of_line, 1 - i // nd, i % 2))
-        leads = low == jnp.where(last_of_line, 1, 0)
-        pl.when(leads & (step < nd - 1))(lambda: wait_planes(piece_at(step + 1)))
+        trails, step = i % 2, i // 2
+        for rows_of, lag in ((first_of_line, 4), (last_of_line, 3)):
+            turns = lagging(nd - 2, lag) + [[side, k] for k in (nd - 2, nd - 1) for side in (0, 1)]
+            trails = jnp.where(rows_of, chain(i, [t for t, _ in turns]), trails)
+            step = jnp.where(rows_of, chain(i, [k for _, k in turns]), step)
+        low = jnp.where(last_of_line, 1 - trails, trails)
+        pl.when((trails == 0) & (step < nd - 1))(lambda: wait_planes(piece_at(step + 1)))
         pl.when(low == 0)(lambda: high_step(step))
         pl.when(low == 1)(lambda: low_step(step))
 

time: 18.8 us -> 18.4 us (0.979)
  Pallas kernels: 17.4 us -> 17 us
    pallas_call x1, Pallas kernels: 17.4 us -> 17 us  [per_device(): pl.pallas_call(functools.partial(render, planes * nd), out_shape=jax.Shap...]
where the time goes in v6:
time: 18.4 us
  Pallas kernels  17 us (92%)
  local copies, waits for them, and re-layouts  0.66 us (4%)
  between operations  0.66 us (4%)
    pallas_call x1, Pallas kernels, per_device(): pl.pallas_call(functools.partial(render, planes * nd), out_shape=jax.Shap...  17 us
    unnamed x1, local copies, waits for them, and re-layouts  0.66 us

profile of v6, /device:TPU:24, one launch (start us, length us, event | category | flops | bytes accessed | tf_op | source)
XLA Modules:
  0.0 18.4 jit_solution(2058738494383237108)
XLA Ops:
  0.7 17.0 %shard_map.37 = f32[4,32,256]{2,1,0:T(8,128)S(1)} custom-call(f32[1]{0:T(128)S(6)} %copy.5.absorption, f32[3]{0:T(128)} %emission_in.1, f32[32,4,16,8,128]{4,3,2,1,0:T(8,128)} %bitcast.3), custom_call_target="tpu_custom_call" | custom-call | tf_op jit(solution)/shard_map/pallas_call | solution.py:401
  17.7 0.7 %copy.6 = f32[4,32,256]{2,1,0:T(8,128)} copy(f32[4,32,256]{2,1,0:T(8,128)S(1)} %shard_map.37) | data formatting | bytes 262144

commit v7 on v6

--- a/solution.py
+++ b/solution.py
@@ -13,7 +13,6 @@
 HIGH, LOW, INNER = range(3)
 LINE = 8
 TOP = 8
-APART = (2, 1, 3, 2, 1, 3, 0, 0)
 
 
 def chain(i, values):
@@ -125,8 +124,10 @@
 
     def order(step, device=d):
         mine = ((step >= chips - 1) & (step < nd - 2)) | (step == nd - 1)
-        core = device % 2
-        return (device // 2 + chain(step, APART)) % chips, jnp.where(mine, core, 1 - core)
+        at, core = device // 2, device % 2
+        other = step % (chips - 1)
+        other = other + jnp.where(other >= at, 1, 0)
+        return jnp.where(step < nd - 2, other, at), jnp.where(mine, core, 1 - core)
 
     def piece_at(step, device=d):
         owner_chip, owner_core = order(step, device)
@@ -152,7 +153,8 @@
         for g in range(groups):
             local_copy(piece, g).start()
 
-    each(nd, start_local)
+    ahead = jnp.where(last_of_line, 2, nd)
+    each(ahead, start_local)
     emission_copy = pltpu.make_async_copy(emission_in, emission, emission_sem)
     emission_copy.start()
 
@@ -202,6 +204,7 @@
     def _():
         pl.semaphore_signal(late_sem, inc=1, device_id={"row": r + 1}, device_id_type=MESH)
         each(nd, lambda step: y_copy(piece_at(step), True).start())
+        each(nd - 2, lambda piece: start_local(piece + 2))
 
     @pl.when(hears)
     def _():

time: 18.4 us -> 17.9 us (0.973)
  Pallas kernels: 17 us -> 16.5 us
    pallas_call x1, Pallas kernels: 17 us -> 16.5 us  [per_device(): pl.pallas_call(functools.partial(render, planes * nd), out_shape=jax.Shap...]
where the time goes in v7:
time: 17.9 us; the launch traced here: 17.8 us
  Pallas kernels  16.5 us (92%)
  local copies, waits for them, and re-layouts  0.66 us (4%)
  between operations  0.66 us (4%)
    pallas_call x1, Pallas kernels, per_device(): pl.pallas_call(functools.partial(render, planes * nd), out_shape=jax.Shap...  16.5 us
    unnamed x1, local copies, waits for them, and re-layouts  0.66 us

profile of v7, /device:TPU:24, one launch (start us, length us, event | category | flops | bytes accessed | tf_op | source)
XLA Modules:
  0.0 17.8 jit_solution(7596081232228339360)
XLA Ops:
  0.7 16.5 %shard_map.37 = f32[4,32,256]{2,1,0:T(8,128)S(1)} custom-call(f32[1]{0:T(128)S(6)} %copy.5.absorption, f32[3]{0:T(128)} %emission_in.1, f32[32,4,16,8,128]{4,3,2,1,0:T(8,128)} %bitcast.3), custom_call_target="tpu_custom_call" | custom-call | tf_op jit(solution)/shard_map/pallas_call | solution.py:404
  17.1 0.7 %copy.6 = f32[4,32,256]{2,1,0:T(8,128)} copy(f32[4,32,256]{2,1,0:T(8,128)S(1)} %shard_map.37) | data formatting | bytes 262144

commit v8 on v7

--- a/solution.py
+++ b/solution.py
@@ -158,24 +158,6 @@
     emission_copy = pltpu.make_async_copy(emission_in, emission, emission_sem)
     emission_copy.start()
 
-    blank = jnp.zeros((planes, rows, LANES), jnp.float32)
-    vol[:, 0, pl.ds(TOP, rows), :] = blank
-    vol[:, tiles + 1, pl.ds(TOP, rows), :] = blank
-
-    def clear_plane(ref):
-        ref[...] = jnp.zeros(ref.shape, jnp.float32)
-
-    def clear_row(y):
-        def one(z):
-            vol[z, :, y, :] = jnp.zeros((tiles + 2, LANES), jnp.float32)
-
-        each(planes, one)
-
-    pl.when(d == 0)(lambda: clear_plane(near))
-    pl.when(d == nd - 1)(lambda: clear_plane(far))
-    pl.when(r == 0)(lambda: clear_row(TOP - 1))
-    pl.when(r == nr - 1)(lambda: clear_row(TOP + rows))
-
     def start_halos(step):
         piece = piece_at(step)
         pl.when(d < nd - 1)(lambda: z_copy(piece_at(step, d + 1), True).start())
@@ -213,6 +195,24 @@
 
     pl.when(greets)(lambda: pl.semaphore_wait(twin_sem, 1))
     each(nd, start_halos)
+
+    blank = jnp.zeros((planes, rows, LANES), jnp.float32)
+    vol[:, 0, pl.ds(TOP, rows), :] = blank
+    vol[:, tiles + 1, pl.ds(TOP, rows), :] = blank
+
+    def clear_plane(ref):
+        ref[...] = jnp.zeros(ref.shape, jnp.float32)
+
+    def clear_row(y):
+        def one(z):
+            vol[z, :, y, :] = jnp.zeros((tiles + 2, LANES), jnp.float32)
+
+        each(planes, one)
+
+    pl.when(d == 0)(lambda: clear_plane(near))
+    pl.when(d == nd - 1)(lambda: clear_plane(far))
+    pl.when(r == 0)(lambda: clear_row(TOP - 1))
+    pl.when(r == nr - 1)(lambda: clear_row(TOP + rows))
 
     rate = absorption[0] * (-math.log2(math.e) / depth_total)
     lane = lax.broadcasted_iota(jnp.int32, (8, LANES), 1)

time: 17.9 us -> 17.8 us (level)
  no operation moved by 1% of the time
where the time goes in v8:
time: 17.8 us; the launch traced here: 17.7 us
  Pallas kernels  16.4 us (92%)
  local copies, waits for them, and re-layouts  0.66 us (4%)
  between operations  0.66 us (4%)
    pallas_call x1, Pallas kernels, per_device(): pl.pallas_call(functools.partial(render, planes * nd), out_shape=jax.Shap...  16.4 us
    unnamed x1, local copies, waits for them, and re-layouts  0.66 us

profile of v8, /device:TPU:24, one launch (start us, length us, event | category | flops | bytes accessed | tf_op | source)
XLA Modules:
  0.0 17.7 jit_solution(10593698200072673022)
XLA Ops:
  0.7 16.4 %shard_map.37 = f32[4,32,256]{2,1,0:T(8,128)S(1)} custom-call(f32[1]{0:T(128)S(6)} %copy.5.absorption, f32[3]{0:T(128)} %emission_in.1, f32[32,4,16,8,128]{4,3,2,1,0:T(8,128)} %bitcast.3), custom_call_target="tpu_custom_call" | custom-call | tf_op jit(solution)/shard_map/pallas_call | solution.py:404
  17.1 0.7 %copy.6 = f32[4,32,256]{2,1,0:T(8,128)} copy(f32[4,32,256]{2,1,0:T(8,128)S(1)} %shard_map.37) | data formatting | bytes 262144
